TPU v7x, 512 devices: a whole 4x4x16 slice. The times are simulated.
512 devices in a mesh: doc: 512 (over y, x, z, core).
Axes of the slice: x: 4, y: 4, z: 16, core: 2. Of those that a mesh axis runs over, the one named last changes fastest.
Arguments:
- documents: bfloat16 [393216, 1024], P('doc'), may hold values from -64 to 64
- labels: bfloat16 [393216, 128], P('doc'), may hold values from -16 to 16
- skeleton: bfloat16 [131072, 1024], P('doc'), may hold values from -64 to 64
- transfer: float32 [2, 4, 256, 256], replicated, may hold values from 0 to 1.5, as said below
- near_peer: int32 [512, 2], P('doc'), may hold values from 0 to 1
- near_live: int32 [512, 2], P('doc'), may hold values 0 or 1
- couple_peer: int32 [512, 3, 2], P('doc'), may hold values from 0 to 1
- couple_live: int32 [512, 3, 2], P('doc'), may hold values 0 or 1
Outputs:
- scores: float32 [393216, 128], P('doc')
Inputs may be any that keep to these rules, and one draw needn't show every extreme that they name: `transfer`: entries are not negative.
All inputs are finite; a program needn't handle non-finite values. No bound on the sum of `near_live` or of `couple_live` on one device may be relied on, other than what follows from the above.
Results may differ from a plain program's by a relative error of at most 0.003.
Values may be sent and summed in bfloat16 or wider, within the bound.
A program may use at most 64 MiB of HBM per device.

v0:
```python
import math

import jax
import jax.numpy as jnp
from jax import lax
from jax.sharding import PartitionSpec as P

eps_value = 1e-06
far_gain = 64.0
highest = lax.Precision.HIGHEST
contract_rows = (((0,), (0,)), ((), ()))
contract_cols = (((1,), (1,)), ((), ()))


def from_behind(value, axis, by):
    devices = lax.axis_size(axis)
    pairs = [(i, i + by) for i in range(devices) if 0 <= i + by < devices]
    return lax.ppermute(value, axis, pairs)


def partner(block, axis, bit):
    count = lax.axis_size(axis)
    route = []
    for low in range(count):
        high = low | 1 << bit
        if high != low and high < count:
            route += [(low, high), (high, low)]
    return lax.ppermute(block, axis, route)


def normalize(row_block):
    widened = row_block.astype(jnp.float32)
    inv_scale = lax.rsqrt(jnp.mean(widened * widened, axis=-1, keepdims=True) + eps_value)
    return (widened * inv_scale).astype(jnp.bfloat16)


def square_sums(row_block):
    widened = row_block.astype(jnp.float32)
    return jnp.sum(widened * widened, axis=1)


def kernel_tile(left_rows, left_sq, right_rows, right_sq):
    cross_dot = lax.dot_general(
        left_rows, right_rows, contract_cols, preferred_element_type=jnp.float32
    )
    feature_width = left_rows.shape[1]
    exponent = (2.0 * feature_width - (left_sq[:, None] + right_sq[None, :] - 2.0 * cross_dot)) / (
        2.0 * math.sqrt(feature_width)
    )
    return jnp.exp(exponent)


def tally_of(peer_codes, live_flags, code_value, in_range):
    matched = live_flags * (peer_codes == code_value).astype(jnp.int32)
    return (jnp.sum(matched) * in_range.astype(jnp.int32)).astype(jnp.float32)


def couple_term(points, points_sq, remote_points, remote_num, remote_den):
    pair_kernel = kernel_tile(points, points_sq, remote_points, square_sums(remote_points)).astype(
        jnp.bfloat16
    )
    return (
        jnp.dot(pair_kernel, remote_num, preferred_element_type=jnp.float32),
        jnp.dot(pair_kernel, remote_den, preferred_element_type=jnp.float32),
    )


def local(documents, labels, skeleton, transfer, near_peer, near_live, couple_peer, couple_live):
    block_count = lax.axis_size("doc")
    my_index = lax.axis_index("doc")
    row_count = documents.shape[0]
    rank_size = skeleton.shape[0]
    label_width = labels.shape[1]
    tier_count = transfer.shape[0]
    docs_norm = normalize(documents)
    docs_sq = square_sums(docs_norm)
    points = normalize(skeleton)
    points_sq = square_sums(points)
    near_before = tally_of(near_peer[0], near_live[0], 0, my_index >= 1)
    near_after = tally_of(near_peer[0], near_live[0], 1, my_index <= block_count - 2)
    own_tile = kernel_tile(docs_norm, docs_sq, docs_norm, docs_sq)
    diagonal = lax.broadcasted_iota(jnp.int32, own_tile.shape, 0) == lax.broadcasted_iota(
        jnp.int32, own_tile.shape, 1
    )
    own_tile = jnp.where(diagonal, 0.0, own_tile).astype(jnp.bfloat16)
    near_num = jnp.dot(own_tile, labels, preferred_element_type=jnp.float32)
    near_den = jnp.sum(own_tile.astype(jnp.float32), axis=1)
    for direction, tally_count in ((1, near_before), (-1, near_after)):
        other_docs, other_labels = from_behind((docs_norm, labels), "doc", direction)
        pair_tile = kernel_tile(docs_norm, docs_sq, other_docs, square_sums(other_docs)).astype(
            jnp.bfloat16
        )
        near_num = near_num + tally_count * jnp.dot(
            pair_tile, other_labels, preferred_element_type=jnp.float32
        )
        near_den = near_den + tally_count * jnp.sum(pair_tile.astype(jnp.float32), axis=1)
    leaf_kernel = kernel_tile(docs_norm, docs_sq, points, points_sq).astype(jnp.bfloat16)
    node_num = (
        lax.dot_general(leaf_kernel, labels, contract_rows, preferred_element_type=jnp.float32)
        / row_count
    )
    node_den = jnp.sum(leaf_kernel.astype(jnp.float32), axis=0) / row_count
    tier_weights = [(node_num, node_den)]
    for height in range(1, tier_count + 1):
        child_slot = my_index // 4 ** (height - 1) % 4
        transfer_mat = lax.dynamic_index_in_dim(transfer[height - 1], child_slot, 0, keepdims=False)
        node_num = 0.25 * lax.dot_general(transfer_mat, node_num, contract_rows, precision=highest)
        node_den = 0.25 * lax.dot_general(transfer_mat, node_den, contract_rows, precision=highest)
        for bit_number in (2 * height - 2, 2 * height - 1):
            sibling_num, sibling_den = partner((node_num, node_den), "doc", bit_number)
            node_num = node_num + sibling_num
            node_den = node_den + sibling_den
        tier_weights.append((node_num, node_den))
    couplings = []
    for height in range(tier_count + 1):
        stride = 4**height
        sent_num = tier_weights[height][0].astype(jnp.bfloat16)
        sent_den = tier_weights[height][1].astype(jnp.bfloat16)
        total_num = jnp.zeros((rank_size, label_width), jnp.float32)
        total_den = jnp.zeros((rank_size,), jnp.float32)
        tally_before = tally_of(
            couple_peer[0, height], couple_live[0, height], 0, my_index >= stride
        )
        tally_after = tally_of(
            couple_peer[0, height], couple_live[0, height], 1, my_index <= block_count - 1 - stride
        )
        for direction in (1, -1):
            tally_count = tally_before if direction == 1 else tally_after
            remote_points, remote_num, remote_den = from_behind(
                (points, sent_num, sent_den), "doc", direction * stride
            )
            term_num, term_den = couple_term(
                points, points_sq, remote_points, remote_num, remote_den
            )
            total_num = total_num + tally_count * term_num
            total_den = total_den + tally_count * term_den
        couplings.append((total_num / rank_size, total_den / rank_size))
    down_num, down_den = couplings[tier_count]
    for height in range(tier_count, 0, -1):
        child_slot = my_index // 4 ** (height - 1) % 4
        transfer_mat = lax.dynamic_index_in_dim(transfer[height - 1], child_slot, 0, keepdims=False)
        down_num = couplings[height - 1][0] + jnp.dot(transfer_mat, down_num, precision=highest)
        down_den = couplings[height - 1][1] + jnp.dot(transfer_mat, down_den, precision=highest)
    kernel_wide = leaf_kernel.astype(jnp.float32)
    far_num = far_gain / rank_size * jnp.dot(kernel_wide, down_num, precision=highest)
    far_den = far_gain / rank_size * jnp.dot(kernel_wide, down_den, precision=highest)
    return (near_num + far_num) / (near_den + far_den)[:, None]


def solution(mesh):
    placed = (
        P("doc", None),
        P("doc", None),
        P("doc", None),
        P(),
        P("doc", None),
        P("doc", None),
        P("doc", None, None),
        P("doc", None, None),
    )
    return jax.shard_map(
        local, mesh=mesh, in_specs=placed, out_specs=P("doc", None), check_vma=False
    )
```

profile of v0, /device:TPU:24, one launch (start us, length us, event | category | flops | bytes accessed | tf_op | source)
XLA Modules:
  0.0 347.8 jit_solution(17553861323057728903)
XLA Ops:
  2.7 18.1 %collective-permute-start.18 = (bf16[256,1024]{1,0:T(8,128)(2,1)S(1)}, bf16[256,1024]{1,0:T(8,128)(2,1)}, u32[]{:S(2)}, u32[]{:S(2)}) collective-permute-start(bf16[256,1024]{1,0:T(8,128)(2,1)S(1)} %get-tuple-element.18), channel_id=1, source_target_pairs={{16,0},{17,1},{18,2},{19,3},{20,4},{21,5},{22,6},{23,7},{24,8},{25... | collective-permute-start | bytes 1572872 | tf_op jit(solution)/shard_map/ppermute | solution.py:18
  36.2 3.7 %convert_reduce_fusion.2 = (f32[768]{0:T(1024)S(1)}, bf16[768,768]{0,1:T(8,128)(2,1)S(1)}) fusion(bf16[768,1024]{1,0:T(8,128)(2,1)} %copy-done.1, f32[768]{0:T(1024)S(1)} %get-tuple-element.15), kind=kOutput, calls=%fused_computation.9 | convolution fusion | flops 1213857024 | bytes 2758656 | tf_op jit(solution)/shard_map/dot_general | solution.py:43
  45.6 19.4 %collective-permute-done.23 = f32[256]{0:T(256)S(1)} collective-permute-done((f32[256]{0:T(256)S(1)}, f32[256]{0:T(256)S(1)}, u32[]{:S(2)}, u32[]{:S(2)}) %collective-permute-start.23) | collective-permute-done | bytes 1056 | tf_op jit(solution)/shard_map/ppermute | solution.py:28
  65.8 4.7 %collective-permute-start.26 = (f32[256]{0:T(256)S(1)}, f32[256]{0:T(256)}, u32[]{:S(2)}, u32[]{:S(2)}) collective-permute-start(f32[256]{0:T(256)S(1)} %broadcast_multiply_fusion), channel_id=1, source_target_pairs={{0,4},{4,0},{1,5},{5,1},{2,6},{6,2},{3,7},{7,3},{8,12},{12,8},{9,1... | collective-permute-start | bytes 3080 | tf_op jit(solution)/shard_map/ppermute | solution.py:28
  86.3 4.8 %collective-permute-start.24 = (bf16[256]{0:T(256)(128)(2,1)}, bf16[256]{0:T(256)(128)(2,1)S(1)}, u32[]{:S(2)}, u32[]{:S(2)}) collective-permute-start(bf16[256]{0:T(256)(128)(2,1)} %get-tuple-element.13), channel_id=1, source_target_pairs={{0,4},{1,5},{2,6},{3,7},{4,8},{5,9},{6,10},{7,11},{8,12},{9,13},{1... | collective-permute-start | bytes 1544 | tf_op jit(solution)/shard_map/ppermute | solution.py:18
  91.1 8.3 %collective-permute-start.29 = (bf16[256]{0:T(256)(128)(2,1)S(1)}, bf16[256]{0:T(256)(128)(2,1)S(1)}, u32[]{:S(2)}, u32[]{:S(2)}) collective-permute-start(bf16[256]{0:T(256)(128)(2,1)S(1)} %add_convert_fusion.2), channel_id=1, source_target_pairs={{16,0},{17,1},{18,2},{19,3},{20,4},{21,5},{22,6},{23,7},{24,8},{25... | collective-permute-start | bytes 1544 | tf_op jit(solution)/shard_map/ppermute | solution.py:18
  99.9 6.3 %collective-permute-start.28 = (bf16[256]{0:T(256)(128)(2,1)S(1)}, bf16[256]{0:T(256)(128)(2,1)S(1)}, u32[]{:S(2)}, u32[]{:S(2)}) collective-permute-start(bf16[256]{0:T(256)(128)(2,1)S(1)} %add_convert_fusion.2), channel_id=1, source_target_pairs={{0,16},{1,17},{2,18},{3,19},{4,20},{5,21},{6,22},{7,23},{8,24},{9,... | collective-permute-start | bytes 1544 | tf_op jit(solution)/shard_map/ppermute | solution.py:18
  110.1 7.9 %collective-permute-start.3 = (bf16[768,128]{1,0:T(8,128)(2,1)S(1)}, bf16[768,128]{1,0:T(8,128)(2,1)S(1)}, u32[]{:S(2)}, u32[]{:S(2)}) collective-permute-start(bf16[768,128]{1,0:T(8,128)(2,1)S(1)} %copy-done.3), channel_id=1, source_target_pairs={{1,0},{2,1},{3,2},{4,3},{5,4},{6,5},{7,6},{8,7},{9,8},{10,9},{11,1... | collective-permute-start | bytes 589832 | tf_op jit(solution)/shard_map/ppermute | solution.py:18
  118.0 5.7 %collective-permute-start.14 = (bf16[256,1024]{1,0:T(8,128)(2,1)S(1)}, bf16[256,1024]{1,0:T(8,128)(2,1)S(1)}, u32[]{:S(2)}, u32[]{:S(2)}) collective-permute-start(bf16[256,1024]{1,0:T(8,128)(2,1)S(1)} %get-tuple-element.18), channel_id=1, source_target_pairs={{0,16},{1,17},{2,18},{3,19},{4,20},{5,21},{6,22},{7,23},{8,24},{9,... | collective-permute-start | bytes 1572872 | tf_op jit(solution)/shard_map/ppermute | solution.py:18
  128.1 43.8 %collective-permute-done.15 = f32[256,128]{1,0:T(8,128)S(1)} collective-permute-done((f32[256,128]{1,0:T(8,128)S(1)}, f32[256,128]{1,0:T(8,128)S(1)}, u32[]{:S(2)}, u32[]{:S(2)}) %collective-permute-start.15) | collective-permute-done | bytes 131104 | tf_op jit(solution)/shard_map/ppermute | solution.py:28
  172.0 9.0 %collective-permute-start.12 = (bf16[256,1024]{1,0:T(8,128)(2,1)S(1)}, bf16[256,1024]{1,0:T(8,128)(2,1)S(1)}, u32[]{:S(2)}, u32[]{:S(2)}) collective-permute-start(bf16[256,1024]{1,0:T(8,128)(2,1)S(1)} %get-tuple-element.18), channel_id=1, source_target_pairs={{4,0},{5,1},{6,2},{7,3},{8,4},{9,5},{10,6},{11,7},{12,8},{13,9},{1... | collective-permute-start | bytes 1572872 | tf_op jit(solution)/shard_map/ppermute | solution.py:18
  185.7 9.2 %collective-permute-start.6 = (bf16[256,1024]{1,0:T(8,128)(2,1)S(1)}, bf16[256,1024]{1,0:T(8,128)(2,1)S(1)}, u32[]{:S(2)}, u32[]{:S(2)}) collective-permute-start(bf16[256,1024]{1,0:T(8,128)(2,1)S(1)} %get-tuple-element.18), channel_id=1, source_target_pairs={{1,0},{2,1},{3,2},{4,3},{5,4},{6,5},{7,6},{8,7},{9,8},{10,9},{11,1... | collective-permute-start | bytes 1572872 | tf_op jit(solution)/shard_map/ppermute | solution.py:18
  195.9 13.3 %collective-permute-done.6 = bf16[256,1024]{1,0:T(8,128)(2,1)S(1)} collective-permute-done((bf16[256,1024]{1,0:T(8,128)(2,1)S(1)}, bf16[256,1024]{1,0:T(8,128)(2,1)S(1)}, u32[]{:S(2)}, u32[]{:S(2)}) %collective-permute-start.6) | collective-permute-done | bytes 524320 | tf_op jit(solution)/shard_map/ppermute | solution.py:18
  211.8 12.3 %collective-permute-done.4 = bf16[256,1024]{1,0:T(8,128)(2,1)S(1)} collective-permute-done((bf16[256,1024]{1,0:T(8,128)(2,1)S(1)}, bf16[256,1024]{1,0:T(8,128)(2,1)S(1)}, u32[]{:S(2)}, u32[]{:S(2)}) %collective-permute-start.4) | collective-permute-done | bytes 524320 | tf_op jit(solution)/shard_map/ppermute | solution.py:18
  230.0 4.0 %collective-permute-start.16 = (f32[256,128]{1,0:T(8,128)S(1)}, f32[256,128]{1,0:T(8,128)S(1)}, u32[]{:S(2)}, u32[]{:S(2)}) collective-permute-start(f32[256,128]{1,0:T(8,128)S(1)} %add.265), channel_id=1, source_target_pairs={{0,8},{8,0},{1,9},{9,1},{2,10},{10,2},{3,11},{11,3},{4,12},{12,4},... | collective-permute-start | bytes 393224 | tf_op jit(solution)/shard_map/ppermute | solution.py:28
  234.7 10.2 %collective-permute-done.16 = f32[256,128]{1,0:T(8,128)S(1)} collective-permute-done((f32[256,128]{1,0:T(8,128)S(1)}, f32[256,128]{1,0:T(8,128)S(1)}, u32[]{:S(2)}, u32[]{:S(2)}) %collective-permute-start.16) | collective-permute-done | bytes 131104 | tf_op jit(solution)/shard_map/ppermute | solution.py:28
  245.0 5.3 %collective-permute-start.2 = (bf16[768,1024]{1,0:T(8,128)(2,1)S(1)}, bf16[768,1024]{1,0:T(8,128)(2,1)S(1)}, u32[]{:S(2)}, u32[]{:S(2)}) collective-permute-start(bf16[768,1024]{1,0:T(8,128)(2,1)S(1)} %copy-done.2), channel_id=1, source_target_pairs={{1,0},{2,1},{3,2},{4,3},{5,4},{6,5},{7,6},{8,7},{9,8},{10,9},{11,1... | collective-permute-start | bytes 4718600 | tf_op jit(solution)/shard_map/ppermute | solution.py:18
  252.8 20.6 %collective-permute-done.13 = bf16[256,128]{1,0:T(8,128)(2,1)S(1)} collective-permute-done((bf16[256,128]{1,0:T(8,128)(2,1)S(1)}, bf16[256,128]{1,0:T(8,128)(2,1)S(1)}, u32[]{:S(2)}, u32[]{:S(2)}) %collective-permute-start.13) | collective-permute-done | bytes 65568 | tf_op jit(solution)/shard_map/ppermute | solution.py:18
  273.3 5.8 %collective-permute-start.19 = (bf16[256,128]{1,0:T(8,128)(2,1)S(1)}, bf16[256,128]{1,0:T(8,128)(2,1)S(1)}, u32[]{:S(2)}, u32[]{:S(2)}) collective-permute-start(bf16[256,128]{1,0:T(8,128)(2,1)S(1)} %add_convert_fusion), channel_id=1, source_target_pairs={{16,0},{17,1},{18,2},{19,3},{20,4},{21,5},{22,6},{23,7},{24,8},{25... | collective-permute-start | bytes 196616 | tf_op jit(solution)/shard_map/ppermute | solution.py:18
  279.8 9.0 %collective-permute-done.19 = bf16[256,128]{1,0:T(8,128)(2,1)S(1)} collective-permute-done((bf16[256,128]{1,0:T(8,128)(2,1)S(1)}, bf16[256,128]{1,0:T(8,128)(2,1)S(1)}, u32[]{:S(2)}, u32[]{:S(2)}) %collective-permute-start.19) | collective-permute-done | bytes 65568 | tf_op jit(solution)/shard_map/ppermute | solution.py:18
  288.8 4.9 %collective-permute-start.17 = (bf16[256,128]{1,0:T(8,128)(2,1)S(1)}, bf16[256,128]{1,0:T(8,128)(2,1)S(1)}, u32[]{:S(2)}, u32[]{:S(2)}) collective-permute-start(bf16[256,128]{1,0:T(8,128)(2,1)S(1)} %add_convert_fusion), channel_id=1, source_target_pairs={{0,16},{1,17},{2,18},{3,19},{4,20},{5,21},{6,22},{7,23},{8,24},{9,... | collective-permute-start | bytes 196616 | tf_op jit(solution)/shard_map/ppermute | solution.py:18
  293.9 12.8 %collective-permute-done.17 = bf16[256,128]{1,0:T(8,128)(2,1)S(1)} collective-permute-done((bf16[256,128]{1,0:T(8,128)(2,1)S(1)}, bf16[256,128]{1,0:T(8,128)(2,1)S(1)}, u32[]{:S(2)}, u32[]{:S(2)}) %collective-permute-start.17) | collective-permute-done | bytes 65568 | tf_op jit(solution)/shard_map/ppermute | solution.py:18
  309.2 8.8 %collective-permute-done.11 = bf16[256,128]{1,0:T(8,128)(2,1)S(1)} collective-permute-done((bf16[256,128]{1,0:T(8,128)(2,1)S(1)}, bf16[256,128]{1,0:T(8,128)(2,1)S(1)}, u32[]{:S(2)}, u32[]{:S(2)}) %collective-permute-start.11) | collective-permute-done | bytes 65568 | tf_op jit(solution)/shard_map/ppermute | solution.py:18
  323.2 20.7 %collective-permute-done = bf16[768,1024]{1,0:T(8,128)(2,1)S(1)} collective-permute-done((bf16[768,1024]{1,0:T(8,128)(2,1)S(1)}, bf16[768,1024]{1,0:T(8,128)(2,1)S(1)}, u32[]{:S(2)}, u32[]{:S(2)}) %collective-permute-start) | collective-permute-done | bytes 1572896 | tf_op jit(solution)/shard_map/ppermute | solution.py:18
  (130 shorter events, 73.8 us)
Async XLA Ops:
  2.7 178.3 %collective-permute-start.18 = (bf16[256,1024]{1,0:T(8,128)(2,1)S(1)}, bf16[256,1024]{1,0:T(8,128)(2,1)}, u32[]{:S(2)}, u32[]{:S(2)}) collective-permute-start(bf16[256,1024]{1,0:T(8,128)(2,1)S(1)} %get-tuple-element.18), channel_id=1, source_target_pairs={{16,0},{17,1},{18,2},{19,3},{20,4},{21,5},{22,6},{23,7},{24,8},{25... | collective-permute-start | bytes 1572872 | tf_op jit(solution)/shard_map/ppermute | solution.py:18
  24.3 62.0 %collective-permute-start.21 = (bf16[256]{0:T(256)(128)(2,1)}, bf16[256]{0:T(256)(128)(2,1)}, u32[]{:S(2)}, u32[]{:S(2)}) collective-permute-start(bf16[256]{0:T(256)(128)(2,1)} %get-tuple-element.21), channel_id=1, source_target_pairs={{1,0},{2,1},{3,2},{4,3},{5,4},{6,5},{7,6},{8,7},{9,8},{10,9},{11,1... | collective-permute-start | bytes 1544 | tf_op jit(solution)/shard_map/ppermute | solution.py:18
  26.2 64.9 %collective-permute-start.20 = (bf16[256]{0:T(256)(128)(2,1)}, bf16[256]{0:T(256)(128)(2,1)}, u32[]{:S(2)}, u32[]{:S(2)}) collective-permute-start(bf16[256]{0:T(256)(128)(2,1)} %get-tuple-element.21), channel_id=1, source_target_pairs={{0,1},{1,2},{2,3},{3,4},{4,5},{5,6},{6,7},{7,8},{8,9},{9,10},{10,1... | collective-permute-start | bytes 1544 | tf_op jit(solution)/shard_map/ppermute | solution.py:18
  34.3 44.5 %collective-permute-start.9 = (f32[256,128]{1,0:T(8,128)S(1)}, f32[256,128]{1,0:T(8,128)S(1)}, u32[]{:S(2)}, u32[]{:S(2)}) collective-permute-start(f32[256,128]{1,0:T(8,128)S(1)} %convolution_multiply_fusion.11), channel_id=1, source_target_pairs={{0,1},{1,0},{2,3},{3,2},{4,5},{5,4},{6,7},{7,6},{8,9},{9,8},{10,11... | collective-permute-start | bytes 393224 | tf_op jit(solution)/shard_map/ppermute | solution.py:28
  42.6 22.3 %collective-permute-start.23 = (f32[256]{0:T(256)S(1)}, f32[256]{0:T(256)S(1)}, u32[]{:S(2)}, u32[]{:S(2)}) collective-permute-start(f32[256]{0:T(256)S(1)} %fusion.61), channel_id=1, source_target_pairs={{0,2},{2,0},{1,3},{3,1},{4,6},{6,4},{5,7},{7,5},{8,10},{10,8},{9,1... | collective-permute-start | bytes 3080 | tf_op jit(solution)/shard_map/ppermute | solution.py:28
  79.4 20.5 %collective-permute-start.25 = (bf16[256]{0:T(256)(128)(2,1)}, bf16[256]{0:T(256)(128)(2,1)}, u32[]{:S(2)}, u32[]{:S(2)}) collective-permute-start(bf16[256]{0:T(256)(128)(2,1)} %get-tuple-element.13), channel_id=1, source_target_pairs={{4,0},{5,1},{6,2},{7,3},{8,4},{9,5},{10,6},{11,7},{12,8},{13,9},{1... | collective-permute-start | bytes 1544 | tf_op jit(solution)/shard_map/ppermute | solution.py:18
  83.3 40.5 %collective-permute-start.10 = (f32[256,128]{1,0:T(8,128)S(1)}, f32[256,128]{1,0:T(8,128)}, u32[]{:S(2)}, u32[]{:S(2)}) collective-permute-start(f32[256,128]{1,0:T(8,128)S(1)} %add.256), channel_id=1, source_target_pairs={{0,2},{2,0},{1,3},{3,1},{4,6},{6,4},{5,7},{7,5},{8,10},{10,8},{9,1... | collective-permute-start | bytes 393224 | tf_op jit(solution)/shard_map/ppermute | solution.py:28
  86.3 21.9 %collective-permute-start.24 = (bf16[256]{0:T(256)(128)(2,1)}, bf16[256]{0:T(256)(128)(2,1)S(1)}, u32[]{:S(2)}, u32[]{:S(2)}) collective-permute-start(bf16[256]{0:T(256)(128)(2,1)} %get-tuple-element.13), channel_id=1, source_target_pairs={{0,4},{1,5},{2,6},{3,7},{4,8},{5,9},{6,10},{7,11},{8,12},{9,13},{1... | collective-permute-start | bytes 1544 | tf_op jit(solution)/shard_map/ppermute | solution.py:18
  91.1 19.0 %collective-permute-start.29 = (bf16[256]{0:T(256)(128)(2,1)S(1)}, bf16[256]{0:T(256)(128)(2,1)S(1)}, u32[]{:S(2)}, u32[]{:S(2)}) collective-permute-start(bf16[256]{0:T(256)(128)(2,1)S(1)} %add_convert_fusion.2), channel_id=1, source_target_pairs={{16,0},{17,1},{18,2},{19,3},{20,4},{21,5},{22,6},{23,7},{24,8},{25... | collective-permute-start | bytes 1544 | tf_op jit(solution)/shard_map/ppermute | solution.py:18
  99.9 18.1 %collective-permute-start.28 = (bf16[256]{0:T(256)(128)(2,1)S(1)}, bf16[256]{0:T(256)(128)(2,1)S(1)}, u32[]{:S(2)}, u32[]{:S(2)}) collective-permute-start(bf16[256]{0:T(256)(128)(2,1)S(1)} %add_convert_fusion.2), channel_id=1, source_target_pairs={{0,16},{1,17},{2,18},{3,19},{4,20},{5,21},{6,22},{7,23},{8,24},{9,... | collective-permute-start | bytes 1544 | tf_op jit(solution)/shard_map/ppermute | solution.py:18
  108.2 238.3 %collective-permute-start.1 = (bf16[768,128]{1,0:T(8,128)(2,1)S(1)}, bf16[768,128]{1,0:T(8,128)(2,1)S(1)}, u32[]{:S(2)}, u32[]{:S(2)}) collective-permute-start(bf16[768,128]{1,0:T(8,128)(2,1)S(1)} %copy-done.3), channel_id=1, source_target_pairs={{0,1},{1,2},{2,3},{3,4},{4,5},{5,6},{6,7},{7,8},{8,9},{9,10},{10,1... | collective-permute-start | bytes 589832 | tf_op jit(solution)/shard_map/ppermute | solution.py:18
  110.1 235.9 %collective-permute-start.3 = (bf16[768,128]{1,0:T(8,128)(2,1)S(1)}, bf16[768,128]{1,0:T(8,128)(2,1)S(1)}, u32[]{:S(2)}, u32[]{:S(2)}) collective-permute-start(bf16[768,128]{1,0:T(8,128)(2,1)S(1)} %copy-done.3), channel_id=1, source_target_pairs={{1,0},{2,1},{3,2},{4,3},{5,4},{6,5},{7,6},{8,7},{9,8},{10,9},{11,1... | collective-permute-start | bytes 589832 | tf_op jit(solution)/shard_map/ppermute | solution.py:18
  118.0 67.7 %collective-permute-start.14 = (bf16[256,1024]{1,0:T(8,128)(2,1)S(1)}, bf16[256,1024]{1,0:T(8,128)(2,1)S(1)}, u32[]{:S(2)}, u32[]{:S(2)}) collective-permute-start(bf16[256,1024]{1,0:T(8,128)(2,1)S(1)} %get-tuple-element.18), channel_id=1, source_target_pairs={{0,16},{1,17},{2,18},{3,19},{4,20},{5,21},{6,22},{7,23},{8,24},{9,... | collective-permute-start | bytes 1572872 | tf_op jit(solution)/shard_map/ppermute | solution.py:18
  125.3 46.7 %collective-permute-start.15 = (f32[256,128]{1,0:T(8,128)S(1)}, f32[256,128]{1,0:T(8,128)S(1)}, u32[]{:S(2)}, u32[]{:S(2)}) collective-permute-start(f32[256,128]{1,0:T(8,128)S(1)} %convolution_multiply_fusion.10), channel_id=1, source_target_pairs={{0,4},{4,0},{1,5},{5,1},{2,6},{6,2},{3,7},{7,3},{8,12},{12,8},{9,1... | collective-permute-start | bytes 393224 | tf_op jit(solution)/shard_map/ppermute | solution.py:28
  172.0 54.7 %collective-permute-start.12 = (bf16[256,1024]{1,0:T(8,128)(2,1)S(1)}, bf16[256,1024]{1,0:T(8,128)(2,1)S(1)}, u32[]{:S(2)}, u32[]{:S(2)}) collective-permute-start(bf16[256,1024]{1,0:T(8,128)(2,1)S(1)} %get-tuple-element.18), channel_id=1, source_target_pairs={{4,0},{5,1},{6,2},{7,3},{8,4},{9,5},{10,6},{11,7},{12,8},{13,9},{1... | collective-permute-start | bytes 1572872 | tf_op jit(solution)/shard_map/ppermute | solution.py:18
  181.0 49.0 %collective-permute-start.8 = (bf16[256,1024]{1,0:T(8,128)(2,1)S(1)}, bf16[256,1024]{1,0:T(8,128)(2,1)S(1)}, u32[]{:S(2)}, u32[]{:S(2)}) collective-permute-start(bf16[256,1024]{1,0:T(8,128)(2,1)S(1)} %get-tuple-element.18), channel_id=1, source_target_pairs={{0,4},{1,5},{2,6},{3,7},{4,8},{5,9},{6,10},{7,11},{8,12},{9,13},{1... | collective-permute-start | bytes 1572872 | tf_op jit(solution)/shard_map/ppermute | solution.py:18
  185.7 23.5 %collective-permute-start.6 = (bf16[256,1024]{1,0:T(8,128)(2,1)S(1)}, bf16[256,1024]{1,0:T(8,128)(2,1)S(1)}, u32[]{:S(2)}, u32[]{:S(2)}) collective-permute-start(bf16[256,1024]{1,0:T(8,128)(2,1)S(1)} %get-tuple-element.18), channel_id=1, source_target_pairs={{1,0},{2,1},{3,2},{4,3},{5,4},{6,5},{7,6},{8,7},{9,8},{10,9},{11,1... | collective-permute-start | bytes 1572872 | tf_op jit(solution)/shard_map/ppermute | solution.py:18
  224.1 26.5 %collective-permute-start.7 = (bf16[256,128]{1,0:T(8,128)(2,1)S(1)}, bf16[256,128]{1,0:T(8,128)(2,1)S(1)}, u32[]{:S(2)}, u32[]{:S(2)}) collective-permute-start(bf16[256,128]{1,0:T(8,128)(2,1)S(1)} %get-tuple-element.23), channel_id=1, source_target_pairs={{1,0},{2,1},{3,2},{4,3},{5,4},{6,5},{7,6},{8,7},{9,8},{10,9},{11,1... | collective-permute-start | bytes 196616 | tf_op jit(solution)/shard_map/ppermute | solution.py:18
  226.7 93.7 %collective-permute-start.5 = (bf16[256,128]{1,0:T(8,128)(2,1)S(1)}, bf16[256,128]{1,0:T(8,128)(2,1)S(1)}, u32[]{:S(2)}, u32[]{:S(2)}) collective-permute-start(bf16[256,128]{1,0:T(8,128)(2,1)S(1)} %get-tuple-element.23), channel_id=1, source_target_pairs={{0,1},{1,2},{2,3},{3,4},{4,5},{5,6},{6,7},{7,8},{8,9},{9,10},{10,1... | collective-permute-start | bytes 196616 | tf_op jit(solution)/shard_map/ppermute | solution.py:18
  245.0 76.2 %collective-permute-start.2 = (bf16[768,1024]{1,0:T(8,128)(2,1)S(1)}, bf16[768,1024]{1,0:T(8,128)(2,1)S(1)}, u32[]{:S(2)}, u32[]{:S(2)}) collective-permute-start(bf16[768,1024]{1,0:T(8,128)(2,1)S(1)} %copy-done.2), channel_id=1, source_target_pairs={{1,0},{2,1},{3,2},{4,3},{5,4},{6,5},{7,6},{8,7},{9,8},{10,9},{11,1... | collective-permute-start | bytes 4718600 | tf_op jit(solution)/shard_map/ppermute | solution.py:18
  250.6 22.7 %collective-permute-start.13 = (bf16[256,128]{1,0:T(8,128)(2,1)S(1)}, bf16[256,128]{1,0:T(8,128)(2,1)S(1)}, u32[]{:S(2)}, u32[]{:S(2)}) collective-permute-start(bf16[256,128]{1,0:T(8,128)(2,1)S(1)} %add_convert_fusion.1), channel_id=1, source_target_pairs={{4,0},{5,1},{6,2},{7,3},{8,4},{9,5},{10,6},{11,7},{12,8},{13,9},{1... | collective-permute-start | bytes 196616 | tf_op jit(solution)/shard_map/ppermute | solution.py:18
  273.3 15.5 %collective-permute-start.19 = (bf16[256,128]{1,0:T(8,128)(2,1)S(1)}, bf16[256,128]{1,0:T(8,128)(2,1)S(1)}, u32[]{:S(2)}, u32[]{:S(2)}) collective-permute-start(bf16[256,128]{1,0:T(8,128)(2,1)S(1)} %add_convert_fusion), channel_id=1, source_target_pairs={{16,0},{17,1},{18,2},{19,3},{20,4},{21,5},{22,6},{23,7},{24,8},{25... | collective-permute-start | bytes 196616 | tf_op jit(solution)/shard_map/ppermute | solution.py:18
  288.8 17.9 %collective-permute-start.17 = (bf16[256,128]{1,0:T(8,128)(2,1)S(1)}, bf16[256,128]{1,0:T(8,128)(2,1)S(1)}, u32[]{:S(2)}, u32[]{:S(2)}) collective-permute-start(bf16[256,128]{1,0:T(8,128)(2,1)S(1)} %add_convert_fusion), channel_id=1, source_target_pairs={{0,16},{1,17},{2,18},{3,19},{4,20},{5,21},{6,22},{7,23},{8,24},{9,... | collective-permute-start | bytes 196616 | tf_op jit(solution)/shard_map/ppermute | solution.py:18
  317.9 25.9 %collective-permute-start = (bf16[768,1024]{1,0:T(8,128)(2,1)S(1)}, bf16[768,1024]{1,0:T(8,128)(2,1)S(1)}, u32[]{:S(2)}, u32[]{:S(2)}) collective-permute-start(bf16[768,1024]{1,0:T(8,128)(2,1)S(1)} %copy-done.2), channel_id=1, source_target_pairs={{0,1},{1,2},{2,3},{3,4},{4,5},{5,6},{6,7},{7,8},{8,9},{9,10},{10,1... | collective-permute-start | bytes 4718600 | tf_op jit(solution)/shard_map/ppermute | solution.py:18
  (16 other events, 261.9 us)
where the time goes:
time: 349 us; the launch traced here: 348 us
  waiting for transfers between devices  171 us (49%)
  starting transfers between devices  132 us (38%)
  matrix products  21.1 us (6%)
  other arithmetic  13.3 us (4%)
  between operations  5.58 us (2%)
  local copies, waits for them, and re-layouts  5.52 us (2%)
    ppermute x22, starting transfers between devices, from_behind(): return lax.ppermute(value, axis, pairs)  108 us
    ppermute x22, waiting for transfers between devices, from_behind(): return lax.ppermute(value, axis, pairs)  97.4 us
    ppermute x8, waiting for transfers between devices, partner(): return lax.ppermute(block, axis, route)  73.5 us
    ppermute x8, starting transfers between devices, partner(): return lax.ppermute(block, axis, route)  23 us
    dot_general x10, matrix products, kernel_tile(): lax.dot_general(left_rows, right_rows, contract_cols, preferred_element_t...  11 us
  transfers between devices with their start and end apart: 30, of which 10 were waited for; matrix products, arithmetic and copies ran while one was open for 10% of the time, Pallas kernels for 0%

commit v1 on v0

v1 whole, which is shorter than its diff:
```python
import functools
import math

import jax
import jax.numpy as jnp
from jax import lax
from jax.experimental import pallas as pl
from jax.experimental.pallas import tpu as pltpu
from jax.sharding import PartitionSpec as P

MESH = pl.DeviceIdType.MESH
f32 = jnp.float32
bf16 = jnp.bfloat16
highest = lax.Precision.HIGHEST
eps_value = 1e-06
far_gain = 64.0
chunk = 256
aug = 144

PTS_UP8, PTS_DOWN8, PTS_UP2, PTS_DOWN2, PTS_DOWN1 = range(5)
DOCS = 5
LABELS = 8
W0 = 9
T1 = 10
T2 = 13
W1, W2 = 16, 17
RET0 = 18
RET1_DOWN, RET1_UP, RET2_DOWN, RET2_UP = 19, 20, 21, 22
NEAR = 23
FLOWS = 26


def dot_nn(a, b, precision=None):
    return lax.dot_general(
        a, b, (((1,), (0,)), ((), ())), precision=precision, preferred_element_type=f32
    )


def dot_nt(a, b, precision=None):
    return lax.dot_general(
        a, b, (((1,), (1,)), ((), ())), precision=precision, preferred_element_type=f32
    )


def normalize(rows):
    wide = rows.astype(f32)
    scale = lax.rsqrt(jnp.mean(wide * wide, axis=-1, keepdims=True) + eps_value)
    return (wide * scale).astype(bf16)


def bias_of(rows):
    wide = rows.astype(f32)
    width = rows.shape[1]
    return (width - jnp.sum(wide * wide, axis=1, keepdims=True)) / (2.0 * math.sqrt(width))


def as_row(column):
    return jnp.broadcast_to(column, (column.shape[0], 128)).T[0:1, :]


def kernel_tile(left, left_bias, right, right_bias_row):
    cross = dot_nt(left, right)
    return jnp.exp(cross * (1.0 / math.sqrt(left.shape[1])) + (left_bias + right_bias_row))


def augmented(labels):
    rows = labels.shape[0]
    turned = labels.astype(f32).T
    ones = (lax.broadcasted_iota(jnp.int32, (aug - labels.shape[1], rows), 0) == 0).astype(f32)
    return jnp.concatenate([turned, ones], axis=0).astype(bf16)


def kernel(
    n,
    docs_in,
    labels_in,
    skel_in,
    transfer_in,
    near_peer,
    near_live,
    couple_peer,
    couple_live,
    out_ref,
    docs,
    docs_bias,
    docs_row,
    lab_t,
    pts,
    leaf,
    docs_r,
    labels_r,
    lab_tr,
    p8,
    p2,
    p1,
    near_t,
    before_t,
    w0_send,
    w0_recv,
    t1_send,
    t1_recv,
    t2_send,
    t2_recv,
    w1_own,
    w1_recv,
    w2_own,
    w2_recv,
    ret0_send,
    ret0_recv,
    ret1_send,
    ret1_recv,
    ret2_send,
    ret2_recv,
    near_send,
    near_recv,
    send_sem,
    recv_sem,
):
    me = lax.axis_index("doc")
    count = docs_in.shape[0]
    rank = skel_in.shape[0]
    pieces = count // chunk

    def at(offset):
        return lax.rem(me + offset + n, n)

    def sibling(bits, unit):
        low = lax.rem(me // unit, 2)
        high = lax.rem(me // (2 * unit), 2)
        step = (1 - 2 * low) * (bits % 2) + (2 - 4 * high) * (bits // 2)
        return me + step * unit

    def send(flow, src, dst, target):
        copy = pltpu.make_async_remote_copy(
            src_ref=src,
            dst_ref=dst,
            send_sem=send_sem.at[flow],
            recv_sem=recv_sem.at[flow],
            device_id=(target,),
            device_id_type=MESH,
        )
        copy.start()
        return copy

    low1 = lax.rem(me, 4) < 2
    low2 = lax.rem(me, 16) < 8
    shift1 = jnp.where(low1, at(-2), at(2))
    shift2 = jnp.where(low2, at(-8), at(8))

    barrier = pltpu.get_barrier_semaphore()
    greeted = [at(1), at(-1), at(2), at(-2), at(8), at(-8)]
    greeted += [sibling(3, 1), sibling(1, 4), sibling(3, 4)]
    for other in greeted:
        pl.semaphore_signal(barrier, inc=1, device_id=(other,), device_id_type=MESH)

    pts[...] = normalize(skel_in[...])
    pl.semaphore_wait(barrier, len(greeted))

    c_up8 = send(PTS_UP8, pts, p8.at[0], at(8))
    c_down8 = send(PTS_DOWN8, pts, p8.at[1], at(-8))
    c_up2 = send(PTS_UP2, pts, p2.at[0], at(2))
    c_down2 = send(PTS_DOWN2, pts, p2.at[1], at(-2))
    c_down1 = send(PTS_DOWN1, pts, p1, at(-1))

    def docs_copy(i):
        rows = pl.ds(pl.multiple_of(i * chunk, chunk), chunk)
        return pltpu.make_async_remote_copy(
            src_ref=docs.at[rows],
            dst_ref=docs_r.at[rows],
            send_sem=send_sem.at[DOCS + i],
            recv_sem=recv_sem.at[DOCS + i],
            device_id=(at(1),),
            device_id_type=MESH,
        )

    def near_copy(i):
        return pltpu.make_async_remote_copy(
            src_ref=near_send.at[i],
            dst_ref=near_recv.at[i],
            send_sem=send_sem.at[NEAR + i],
            recv_sem=recv_sem.at[NEAR + i],
            device_id=(at(-1),),
            device_id_type=MESH,
        )

    c_labels = send(LABELS, labels_in, labels_r, at(1))

    @pl.loop(0, pieces)
    def _(i):
        rows = pl.ds(pl.multiple_of(i * chunk, chunk), chunk)
        docs[rows, :] = normalize(docs_in[rows, :])
        docs_copy(i).start()

    lab_t[...] = augmented(labels_in[...])
    pts_bias = bias_of(pts[...])
    pts_row = as_row(pts_bias)

    @pl.loop(0, pieces)
    def _(i):
        rows = pl.ds(pl.multiple_of(i * chunk, chunk), chunk)
        block = docs[rows, :]
        bias = bias_of(block)
        docs_bias[rows, :] = bias
        docs_row[:, rows] = as_row(bias)
        leaf[rows, :] = kernel_tile(block, bias, pts[...], pts_row).astype(bf16)

    w0 = dot_nn(lab_t[...], leaf[...]) * (1.0 / count)
    w0_send[...] = w0.astype(bf16)
    c_w0 = send(W0, w0_send, w0_recv, at(-1))
    child1 = lax.rem(me, 4)
    child2 = lax.rem(me // 4, 4)
    t1 = 0.25 * dot_nn(w0, transfer_in[0, child1], highest)
    t1_send[...] = t1.astype(bf16)
    c_t1 = [send(T1 + j, t1_send, t1_recv.at[j], sibling(j + 1, 1)) for j in range(3)]

    near_t[...] = jnp.zeros_like(near_t)

    @pl.loop(0, pieces)
    def _(i):
        rows = pl.ds(pl.multiple_of(i * chunk, chunk), chunk)
        tile = kernel_tile(docs[rows, :], docs_bias[rows, :], docs[...], docs_row[...])
        row_ids = lax.broadcasted_iota(jnp.int32, tile.shape, 0) + i * chunk
        col_ids = lax.broadcasted_iota(jnp.int32, tile.shape, 1)
        tile = jnp.where(row_ids == col_ids, 0.0, tile).astype(bf16)
        near_t[...] += dot_nn(lab_t[:, rows], tile)

    for copy in c_t1:
        copy.wait_recv()
    w1 = t1 + t1_recv[0].astype(f32) + (t1_recv[1].astype(f32) + t1_recv[2].astype(f32))
    w1_own[...] = w1.astype(bf16)
    c_w1 = send(W1, w1_own, w1_recv, shift1)
    t2 = 0.25 * dot_nn(w1, transfer_in[1, child2], highest)
    t2_send[...] = t2.astype(bf16)
    c_t2 = [send(T2 + j, t2_send, t2_recv.at[j], sibling(j + 1, 4)) for j in range(3)]

    c_down1.wait_recv()
    c_w0.wait_recv()
    pair = kernel_tile(pts[...], pts_bias, p1[...], as_row(bias_of(p1[...]))).astype(bf16)
    ret0_send[...] = dot_nn(w0_send[...], pair).astype(bf16)
    c_ret0 = send(RET0, ret0_send, ret0_recv, at(1))
    after0 = dot_nt(w0_recv[...], pair)

    for copy in c_t2:
        copy.wait_recv()
    w2 = t2 + t2_recv[0].astype(f32) + (t2_recv[1].astype(f32) + t2_recv[2].astype(f32))
    w2_own[...] = w2.astype(bf16)
    c_w2 = send(W2, w2_own, w2_recv, shift2)

    c_up2.wait_recv()
    c_down2.wait_recv()
    c_w1.wait_recv()
    pair = kernel_tile(
        p2[0], bias_of(p2[0]), p2[1], as_row(bias_of(p2[1]))
    ).astype(bf16)
    w_before = jnp.where(low1, w1_recv[...], w1_own[...])
    w_after = jnp.where(low1, w1_own[...], w1_recv[...])
    ret1_send[0] = dot_nt(w_after, pair).astype(bf16)
    ret1_send[1] = dot_nn(w_before, pair).astype(bf16)
    c_ret1 = [
        send(RET1_DOWN, ret1_send.at[0], ret1_recv.at[0], at(-2)),
        send(RET1_UP, ret1_send.at[1], ret1_recv.at[1], at(2)),
    ]

    c_labels.wait_recv()
    lab_tr[...] = augmented(labels_r[...])
    before_t[...] = jnp.zeros_like(before_t)

    @pl.loop(0, pieces)
    def _(i):
        rows = pl.ds(pl.multiple_of(i * chunk, chunk), chunk)
        docs_copy(i).wait_recv()
        block = docs_r[rows, :]
        tile = kernel_tile(block, bias_of(block), docs[...], docs_row[...]).astype(bf16)
        near_send[i] = dot_nt(lab_t[...], tile).astype(bf16)
        near_copy(i).start()
        before_t[...] += dot_nn(lab_tr[:, rows], tile)

    c_up8.wait_recv()
    c_down8.wait_recv()
    c_w2.wait_recv()
    pair = kernel_tile(
        p8[0], bias_of(p8[0]), p8[1], as_row(bias_of(p8[1]))
    ).astype(bf16)
    w_before = jnp.where(low2, w2_recv[...], w2_own[...])
    w_after = jnp.where(low2, w2_own[...], w2_recv[...])
    ret2_send[0] = dot_nt(w_after, pair).astype(bf16)
    ret2_send[1] = dot_nn(w_before, pair).astype(bf16)
    c_ret2 = [
        send(RET2_DOWN, ret2_send.at[0], ret2_recv.at[0], at(-8)),
        send(RET2_UP, ret2_send.at[1], ret2_recv.at[1], at(8)),
    ]

    def tally(peer, live, code, inside):
        total = jnp.int32(0)
        for p, v in zip(peer, live):
            total = total + v * (p == code).astype(jnp.int32)
        return (total * inside.astype(jnp.int32)).astype(f32)

    def tallies(peer, live, stride):
        return (
            tally(peer, live, 0, me >= stride),
            tally(peer, live, 1, me <= n - 1 - stride),
        )

    slots = near_peer.shape[1]
    near_before, near_after = tallies(
        [near_peer[0, j] for j in range(slots)], [near_live[0, j] for j in range(slots)], 1
    )
    couple = [
        tallies(
            [couple_peer[0, level, j] for j in range(slots)],
            [couple_live[0, level, j] for j in range(slots)],
            4**level,
        )
        for level in range(3)
    ]

    c_ret0.wait_recv()
    far0 = (couple[0][0] * ret0_recv[...].astype(f32) + couple[0][1] * after0) / rank
    for copy in c_ret1:
        copy.wait_recv()
    far1 = (
        couple[1][1] * ret1_recv[0].astype(f32) + couple[1][0] * ret1_recv[1].astype(f32)
    ) / rank

    @pl.loop(0, pieces)
    def _(i):
        rows = pl.ds(pl.multiple_of(i * chunk, chunk), chunk)
        near_copy(i).wait_recv()
        near_t[:, rows] += (
            near_before * before_t[:, rows] + near_after * near_recv[i].astype(f32)
        )

    for copy in c_ret2:
        copy.wait_recv()
    down = (
        couple[2][1] * ret2_recv[0].astype(f32) + couple[2][0] * ret2_recv[1].astype(f32)
    ) / rank
    down = far1 + dot_nt(down, transfer_in[1, child2], highest)
    down = far0 + dot_nt(down, transfer_in[0, child1], highest)
    down_high = down.astype(bf16)
    down_low = (down - down_high.astype(f32)).astype(bf16)
    far = dot_nt(down_high, leaf[...]) + dot_nt(down_low, leaf[...])
    total = near_t[...] + (far_gain / rank) * far
    width = labels_in.shape[1]
    out_ref[...] = (total[:width] / total[width : width + 1]).T

    for copy in [c_up8, c_down8, c_up2, c_down2, c_down1, c_labels, c_w0, c_w1, c_w2, c_ret0]:
        copy.wait_send()
    for copy in c_t1 + c_t2 + c_ret1 + c_ret2:
        copy.wait_send()

    @pl.loop(0, pieces)
    def _(i):
        docs_copy(i).wait_send()
        near_copy(i).wait_send()


def solution(mesh):
    n = mesh.shape["doc"]

    def local(documents, labels, skeleton, transfer, near_peer, near_live, couple_peer, couple_live):
        count, depth = documents.shape
        width = labels.shape[1]
        rank = skeleton.shape[0]
        pieces = count // chunk
        node = lambda *lead: pltpu.VMEM((*lead, aug, rank), bf16)
        vmem = pl.BlockSpec(memory_space=pltpu.VMEM)
        smem = pl.BlockSpec(memory_space=pltpu.SMEM)
        return pl.pallas_call(
            functools.partial(kernel, n),
            out_shape=jax.ShapeDtypeStruct((count, width), f32),
            in_specs=[vmem] * 4 + [smem] * 4,
            out_specs=vmem,
            scratch_shapes=[
                pltpu.VMEM((count, depth), bf16),
                pltpu.VMEM((count, 1), f32),
                pltpu.VMEM((1, count), f32),
                pltpu.VMEM((aug, count), bf16),
                pltpu.VMEM((rank, depth), bf16),
                pltpu.VMEM((count, rank), bf16),
                pltpu.VMEM((count, depth), bf16),
                pltpu.VMEM((count, width), bf16),
                pltpu.VMEM((aug, count), bf16),
                pltpu.VMEM((2, rank, depth), bf16),
                pltpu.VMEM((2, rank, depth), bf16),
                pltpu.VMEM((rank, depth), bf16),
                pltpu.VMEM((aug, count), f32),
                pltpu.VMEM((aug, count), f32),
                node(),
                node(),
                node(),
                node(3),
                node(),
                node(3),
                node(),
                node(),
                node(),
                node(),
                node(),
                node(),
                node(2),
                node(2),
                node(2),
                node(2),
                node(pieces),
                node(pieces),
                pltpu.SemaphoreType.DMA((FLOWS,)),
                pltpu.SemaphoreType.DMA((FLOWS,)),
            ],
            compiler_params=pltpu.CompilerParams(
                collective_id=0, has_side_effects=True, vmem_limit_bytes=48 * 2**20
            ),
        )(documents, labels, skeleton, transfer, near_peer, near_live, couple_peer, couple_live)

    placed = (
        P("doc", None),
        P("doc", None),
        P("doc", None),
        P(),
        P("doc", None),
        P("doc", None),
        P("doc", None, None),
        P("doc", None, None),
    )
    return jax.shard_map(
        local, mesh=mesh, in_specs=placed, out_specs=P("doc", None), check_vma=False
    )
```

time: 349 us -> 136 us (0.39)
  the two profiles are of different devices: /device:TPU:24 before, /device:TPU:32 now
where the time goes in v1:
time: 136 us
  Pallas kernels  128 us (94%)
  local copies, waits for them, and re-layouts  8.55 us (6%)
    pallas_call x1, Pallas kernels, local(): pl.pallas_call(functools.partial(kernel, n), out_shape=jax.ShapeDtypeStru...  128 us
    unnamed x15, local copies, waits for them, and re-layouts  8.55 us

profile of v1, /device:TPU:32, one launch (start us, length us, event | category | flops | bytes accessed | tf_op | source)
XLA Modules:
  0.0 136.1 jit_solution(12540836378475315036)
XLA Ops:
  0.0 0.8 copy.9.couple_peer
  0.8 0.8 copy.10.couple_live
  1.5 0.0 copy-start
  1.5 1.6 %copy-done = f32[2,4,256,256]{3,2,1,0:T(8,128)S(1)} copy-done((f32[2,4,256,256]{3,2,1,0:T(8,128)S(1)}, f32[2,4,256,256]{3,2,1,0:T(8,128)}, u32[]{:S(2)}) %copy-start) | copy-done | bytes 2097176
  3.1 0.0 copy-start.1
  3.1 1.4 %copy-done.1 = bf16[768,1024]{1,0:T(8,128)(2,1)S(1)} copy-done((bf16[768,1024]{1,0:T(8,128)(2,1)S(1)}, bf16[768,1024]{1,0:T(8,128)(2,1)}, u32[]{:S(2)}) %copy-start.1) | copy-done | bytes 1572888
  4.5 0.0 copy-start.2
  4.5 1.0 copy-done.2
  5.6 0.0 copy-start.3
  5.6 0.9 copy-done.3
  6.5 0.0 copy-start.4
  6.5 0.7 copy-done.4
  7.2 0.0 copy-start.5
  7.2 0.7 copy-done.5
  7.8 127.5 %shard_map.82 = f32[768,128]{1,0:T(8,128)S(1)} custom-call(bf16[768,1024]{1,0:T(8,128)(2,1)S(1)} %copy-done.1, bf16[768,128]{1,0:T(8,128)(2,1)S(1)} %copy-done.3, bf16[256,1024]{1,0:T(8,128)(2,1)S(1)} %copy-done.2, f32[2,4,256,256]{3,2,1,0:T(8,128)S(1)} %copy-done, s32[1,2]{1,0:T(1,128)S(1)} %copy-done.4, s32[1,2]{1,0:T(1,128)S(1)} %copy-done.5, ...), custom_call_target="tpu_custom_call" | custom-call | tf_op jit(solution)/shard_map/pallas_call | solution.py:370
  135.3 0.7 copy.12
Async XLA Ops:
  1.5 1.6 %copy-start = (f32[2,4,256,256]{3,2,1,0:T(8,128)S(1)}, f32[2,4,256,256]{3,2,1,0:T(8,128)}, u32[]{:S(2)}) copy-start(f32[2,4,256,256]{3,2,1,0:T(8,128)} %transfer_in.1) | copy-start | bytes 6291460
  3.1 1.4 %copy-start.1 = (bf16[768,1024]{1,0:T(8,128)(2,1)S(1)}, bf16[768,1024]{1,0:T(8,128)(2,1)}, u32[]{:S(2)}) copy-start(bf16[768,1024]{1,0:T(8,128)(2,1)} %docs_in.1) | copy-start | bytes 4718596
  4.5 1.0 copy-start.2
  5.6 0.9 copy-start.3
  6.5 0.7 copy-start.4
  7.2 0.7 copy-start.5

commit v2 on v1

--- a/solution.py
+++ b/solution.py
@@ -17,17 +17,31 @@
 chunk = 256
 aug = 144
 
-PTS_UP8, PTS_DOWN8, PTS_UP2, PTS_DOWN2, PTS_DOWN1 = range(5)
+PTS_UP8, PTS_DOWN8, PTS_UP2, PTS_DOWN, PTS_DOWN1 = range(5)
 DOCS = 5
 LABELS = 8
 W0 = 9
 T1 = 10
-T2 = 13
-W1, W2 = 16, 17
-RET0 = 18
-RET1_DOWN, RET1_UP, RET2_DOWN, RET2_UP = 19, 20, 21, 22
-NEAR = 23
-FLOWS = 26
+SHARE1 = 13
+W1 = 16
+T2 = 17
+SHARE2 = 20
+SHIFT2 = 23
+SHARE_NEXT = 24
+RET0 = 27
+RET1_DOWN, RET1_UP, RET2_DOWN, RET2_UP = 28, 29, 30, 31
+NEAR = 32
+FLOWS = 35
+
+part = 48
+step_rows = 32
+
+IN_SKEL = 0
+IN_LABELS = 1
+IN_TRANSFER = 2
+IN_LISTS = 3
+IN_DOCS = 7
+INPUTS = 10
 
 
 def dot_nn(a, b, precision=None):
@@ -70,8 +84,24 @@
     return jnp.concatenate([turned, ones], axis=0).astype(bf16)
 
 
+def whole(parts):
+    last = parts.shape[0] - 1
+    return jnp.concatenate(
+        [parts[j, :step_rows] for j in range(last)] + [parts[last]], axis=0
+    )
+
+
 def kernel(
     n,
+    docs_hbm,
+    labels_hbm,
+    skel_hbm,
+    transfer_hbm,
+    near_peer_hbm,
+    near_live_hbm,
+    couple_peer_hbm,
+    couple_live_hbm,
+    out_ref,
     docs_in,
     labels_in,
     skel_in,
@@ -80,7 +110,6 @@
     near_live,
     couple_peer,
     couple_live,
-    out_ref,
     docs,
     docs_bias,
     docs_row,
@@ -97,14 +126,16 @@
     before_t,
     w0_send,
     w0_recv,
+    t1_sum,
     t1_send,
     t1_recv,
+    w1_parts,
+    w1_own,
+    w1_next,
     t2_send,
     t2_recv,
-    w1_own,
-    w1_recv,
-    w2_own,
-    w2_recv,
+    w2_parts,
+    w2_next,
     ret0_send,
     ret0_recv,
     ret1_send,
@@ -113,6 +144,7 @@
     ret2_recv,
     near_send,
     near_recv,
+    in_sem,
     send_sem,
     recv_sem,
 ):
@@ -120,15 +152,48 @@
     count = docs_in.shape[0]
     rank = skel_in.shape[0]
     pieces = count // chunk
+    core = lax.rem(me, 2)
+    quarter = lax.rem(me, 4)
+
+    def piece(i):
+        return pl.ds(pl.multiple_of(i * chunk, chunk), chunk)
+
+    def part_rows(j):
+        return pl.ds(pl.multiple_of(j * step_rows, step_rows), part)
+
+    def fetch(slot, src, dst):
+        return pltpu.make_async_copy(src, dst, in_sem.at[slot])
+
+    def docs_fetch(i):
+        return fetch(IN_DOCS + i, docs_hbm.at[piece(i)], docs_in.at[piece(i)])
+
+    f_skel = fetch(IN_SKEL, skel_hbm, skel_in)
+    f_skel.start()
+    for i in range(pieces):
+        docs_fetch(i).start()
+    f_labels = fetch(IN_LABELS, labels_hbm, labels_in)
+    f_labels.start()
+    f_transfer = fetch(IN_TRANSFER, transfer_hbm, transfer_in)
+    f_transfer.start()
+    f_lists = [
+        fetch(IN_LISTS, near_peer_hbm, near_peer),
+        fetch(IN_LISTS + 1, near_live_hbm, near_live),
+        fetch(IN_LISTS + 2, couple_peer_hbm, couple_peer),
+        fetch(IN_LISTS + 3, couple_live_hbm, couple_live),
+    ]
+    for f in f_lists:
+        f.start()
 
     def at(offset):
         return lax.rem(me + offset + n, n)
 
+    def flipped(place, bits):
+        low = lax.rem(place, 2)
+        high = lax.rem(place // 2, 2)
+        return (1 - 2 * low) * (bits % 2) + (2 - 4 * high) * (bits // 2)
+
     def sibling(bits, unit):
-        low = lax.rem(me // unit, 2)
-        high = lax.rem(me // (2 * unit), 2)
-        step = (1 - 2 * low) * (bits % 2) + (2 - 4 * high) * (bits // 2)
-        return me + step * unit
+        return me + flipped(me // unit, bits) * unit
 
     def send(flow, src, dst, target):
         copy = pltpu.make_async_remote_copy(
@@ -142,31 +207,58 @@
         copy.start()
         return copy
 
-    low1 = lax.rem(me, 4) < 2
+    even = core == 0
+    odd = core == 1
+    next1 = jnp.where(even, jnp.where(quarter < 2, at(-2), at(2)), at(-4))
+    low1 = jnp.logical_and(even, quarter < 2)
     low2 = lax.rem(me, 16) < 8
-    shift1 = jnp.where(low1, at(-2), at(2))
-    shift2 = jnp.where(low2, at(-8), at(8))
+    next2 = jnp.where(low2, at(-8), at(8))
 
     barrier = pltpu.get_barrier_semaphore()
-    greeted = [at(1), at(-1), at(2), at(-2), at(8), at(-8)]
-    greeted += [sibling(3, 1), sibling(1, 4), sibling(3, 4)]
+    greeted = [at(1), at(-1), at(2), at(-2), at(4), at(-4), at(8), at(-8)]
+    greeted += [sibling(3, 1), sibling(3, 4)]
     for other in greeted:
         pl.semaphore_signal(barrier, inc=1, device_id=(other,), device_id_type=MESH)
 
+    f_skel.wait()
     pts[...] = normalize(skel_in[...])
     pl.semaphore_wait(barrier, len(greeted))
 
     c_up8 = send(PTS_UP8, pts, p8.at[0], at(8))
     c_down8 = send(PTS_DOWN8, pts, p8.at[1], at(-8))
-    c_up2 = send(PTS_UP2, pts, p2.at[0], at(2))
-    c_down2 = send(PTS_DOWN2, pts, p2.at[1], at(-2))
+
+    def up2_copy():
+        return pltpu.make_async_remote_copy(
+            src_ref=pts,
+            dst_ref=p2.at[0],
+            send_sem=send_sem.at[PTS_UP2],
+            recv_sem=recv_sem.at[PTS_UP2],
+            device_id=(at(2),),
+            device_id_type=MESH,
+        )
+
+    def ret1_down_copy():
+        return pltpu.make_async_remote_copy(
+            src_ref=ret1_send.at[0],
+            dst_ref=ret1_recv.at[0],
+            send_sem=send_sem.at[RET1_DOWN],
+            recv_sem=recv_sem.at[RET1_DOWN],
+            device_id=(at(-2),),
+            device_id_type=MESH,
+        )
+
+    c_down = send(PTS_DOWN, pts, p2.at[1], jnp.where(even, at(-2), at(-4)))
+
+    @pl.when(even)
+    def _():
+        up2_copy().start()
+
     c_down1 = send(PTS_DOWN1, pts, p1, at(-1))
 
     def docs_copy(i):
-        rows = pl.ds(pl.multiple_of(i * chunk, chunk), chunk)
         return pltpu.make_async_remote_copy(
-            src_ref=docs.at[rows],
-            dst_ref=docs_r.at[rows],
+            src_ref=docs.at[piece(i)],
+            dst_ref=docs_r.at[piece(i)],
             send_sem=send_sem.at[DOCS + i],
             recv_sem=recv_sem.at[DOCS + i],
             device_id=(at(1),),
@@ -183,21 +275,21 @@
             device_id_type=MESH,
         )
 
-    c_labels = send(LABELS, labels_in, labels_r, at(1))
-
     @pl.loop(0, pieces)
     def _(i):
-        rows = pl.ds(pl.multiple_of(i * chunk, chunk), chunk)
-        docs[rows, :] = normalize(docs_in[rows, :])
+        docs_fetch(i).wait()
+        docs[piece(i), :] = normalize(docs_in[piece(i), :])
         docs_copy(i).start()
 
+    f_labels.wait()
+    c_labels = send(LABELS, labels_in, labels_r, at(1))
     lab_t[...] = augmented(labels_in[...])
     pts_bias = bias_of(pts[...])
     pts_row = as_row(pts_bias)
 
     @pl.loop(0, pieces)
     def _(i):
-        rows = pl.ds(pl.multiple_of(i * chunk, chunk), chunk)
+        rows = piece(i)
         block = docs[rows, :]
         bias = bias_of(block)
         docs_bias[rows, :] = bias
@@ -207,17 +299,27 @@
     w0 = dot_nn(lab_t[...], leaf[...]) * (1.0 / count)
     w0_send[...] = w0.astype(bf16)
     c_w0 = send(W0, w0_send, w0_recv, at(-1))
-    child1 = lax.rem(me, 4)
+
+    f_transfer.wait()
     child2 = lax.rem(me // 4, 4)
-    t1 = 0.25 * dot_nn(w0, transfer_in[0, child1], highest)
+    t1 = 0.25 * dot_nn(w0, transfer_in[0, quarter], highest)
+    t1_sum[...] = t1
     t1_send[...] = t1.astype(bf16)
-    c_t1 = [send(T1 + j, t1_send, t1_recv.at[j], sibling(j + 1, 1)) for j in range(3)]
+    c_t1 = [
+        send(
+            T1 + j,
+            t1_send.at[part_rows(quarter + flipped(quarter, j + 1))],
+            t1_recv.at[j],
+            sibling(j + 1, 1),
+        )
+        for j in range(3)
+    ]
 
     near_t[...] = jnp.zeros_like(near_t)
 
     @pl.loop(0, pieces)
     def _(i):
-        rows = pl.ds(pl.multiple_of(i * chunk, chunk), chunk)
+        rows = piece(i)
         tile = kernel_tile(docs[rows, :], docs_bias[rows, :], docs[...], docs_row[...])
         row_ids = lax.broadcasted_iota(jnp.int32, tile.shape, 0) + i * chunk
         col_ids = lax.broadcasted_iota(jnp.int32, tile.shape, 1)
@@ -226,9 +328,14 @@
 
     for copy in c_t1:
         copy.wait_recv()
-    w1 = t1 + t1_recv[0].astype(f32) + (t1_recv[1].astype(f32) + t1_recv[2].astype(f32))
-    w1_own[...] = w1.astype(bf16)
-    c_w1 = send(W1, w1_own, w1_recv, shift1)
+    w1 = (t1_sum[part_rows(quarter), :] + t1_recv[0].astype(f32)) + (
+        t1_recv[1].astype(f32) + t1_recv[2].astype(f32)
+    )
+    w1_parts[quarter] = w1.astype(bf16)
+    c_share1 = [
+        send(SHARE1 + j, w1_parts.at[quarter], w1_parts.at[quarter], sibling(j + 1, 1))
+        for j in range(3)
+    ]
     t2 = 0.25 * dot_nn(w1, transfer_in[1, child2], highest)
     t2_send[...] = t2.astype(bf16)
     c_t2 = [send(T2 + j, t2_send, t2_recv.at[j], sibling(j + 1, 4)) for j in range(3)]
@@ -242,24 +349,54 @@
 
     for copy in c_t2:
         copy.wait_recv()
-    w2 = t2 + t2_recv[0].astype(f32) + (t2_recv[1].astype(f32) + t2_recv[2].astype(f32))
-    w2_own[...] = w2.astype(bf16)
-    c_w2 = send(W2, w2_own, w2_recv, shift2)
-
-    c_up2.wait_recv()
-    c_down2.wait_recv()
+    w2 = (t2 + t2_recv[0].astype(f32)) + (t2_recv[1].astype(f32) + t2_recv[2].astype(f32))
+    w2_parts[quarter] = w2.astype(bf16)
+    c_shift2 = send(SHIFT2, w2_parts.at[quarter], w2_next.at[quarter], next2)
+    c_share2 = [
+        send(SHARE2 + j, w2_parts.at[quarter], w2_parts.at[quarter], sibling(j + 1, 1))
+        for j in range(3)
+    ]
+
+    for copy in c_share1:
+        copy.wait_recv()
+    w1_own[...] = whole(w1_parts)
+    c_w1 = send(W1, w1_own, w1_next, next1)
+
+    c_shift2.wait_recv()
+    c_share_next = [
+        send(SHARE_NEXT + j, w2_next.at[quarter], w2_next.at[quarter], sibling(j + 1, 1))
+        for j in range(3)
+    ]
+
+    c_down.wait_recv()
+
+    @pl.when(even)
+    def _():
+        up2_copy().wait_recv()
+
+    @pl.when(odd)
+    def _():
+        p2[0] = pts[...]
+
     c_w1.wait_recv()
     pair = kernel_tile(
         p2[0], bias_of(p2[0]), p2[1], as_row(bias_of(p2[1]))
     ).astype(bf16)
-    w_before = jnp.where(low1, w1_recv[...], w1_own[...])
-    w_after = jnp.where(low1, w1_own[...], w1_recv[...])
+    w_before = jnp.where(low1, w1_next[...], w1_own[...])
+    w_after = jnp.where(low1, w1_own[...], w1_next[...])
     ret1_send[0] = dot_nt(w_after, pair).astype(bf16)
     ret1_send[1] = dot_nn(w_before, pair).astype(bf16)
-    c_ret1 = [
-        send(RET1_DOWN, ret1_send.at[0], ret1_recv.at[0], at(-2)),
-        send(RET1_UP, ret1_send.at[1], ret1_recv.at[1], at(2)),
-    ]
+    c_ret1 = send(
+        RET1_UP, ret1_send.at[1], ret1_recv.at[1], jnp.where(even, at(2), at(4))
+    )
+
+    @pl.when(even)
+    def _():
+        ret1_down_copy().start()
+
+    @pl.when(odd)
+    def _():
+        ret1_recv[0] = ret1_send[0]
 
     c_labels.wait_recv()
     lab_tr[...] = augmented(labels_r[...])
@@ -267,7 +404,7 @@
 
     @pl.loop(0, pieces)
     def _(i):
-        rows = pl.ds(pl.multiple_of(i * chunk, chunk), chunk)
+        rows = piece(i)
         docs_copy(i).wait_recv()
         block = docs_r[rows, :]
         tile = kernel_tile(block, bias_of(block), docs[...], docs_row[...]).astype(bf16)
@@ -275,14 +412,17 @@
         near_copy(i).start()
         before_t[...] += dot_nn(lab_tr[:, rows], tile)
 
+    for copy in c_share2 + c_share_next:
+        copy.wait_recv()
+    own2 = whole(w2_parts)
+    other2 = whole(w2_next)
+    w_before = jnp.where(low2, other2, own2)
+    w_after = jnp.where(low2, own2, other2)
     c_up8.wait_recv()
     c_down8.wait_recv()
-    c_w2.wait_recv()
     pair = kernel_tile(
         p8[0], bias_of(p8[0]), p8[1], as_row(bias_of(p8[1]))
     ).astype(bf16)
-    w_before = jnp.where(low2, w2_recv[...], w2_own[...])
-    w_after = jnp.where(low2, w2_own[...], w2_recv[...])
     ret2_send[0] = dot_nt(w_after, pair).astype(bf16)
     ret2_send[1] = dot_nn(w_before, pair).astype(bf16)
     c_ret2 = [
@@ -302,14 +442,16 @@
             tally(peer, live, 1, me <= n - 1 - stride),
         )
 
+    for f in f_lists:
+        f.wait()
     slots = near_peer.shape[1]
     near_before, near_after = tallies(
         [near_peer[0, j] for j in range(slots)], [near_live[0, j] for j in range(slots)], 1
     )
     couple = [
         tallies(
-            [couple_peer[0, level, j] for j in range(slots)],
-            [couple_live[0, level, j] for j in range(slots)],
+            [couple_peer[0, j, level] for j in range(slots)],
+            [couple_live[0, j, level] for j in range(slots)],
             4**level,
         )
         for level in range(3)
@@ -317,15 +459,19 @@
 
     c_ret0.wait_recv()
     far0 = (couple[0][0] * ret0_recv[...].astype(f32) + couple[0][1] * after0) / rank
-    for copy in c_ret1:
-        copy.wait_recv()
+    c_ret1.wait_recv()
+
+    @pl.when(even)
+    def _():
+        ret1_down_copy().wait_recv()
+
     far1 = (
         couple[1][1] * ret1_recv[0].astype(f32) + couple[1][0] * ret1_recv[1].astype(f32)
     ) / rank
 
     @pl.loop(0, pieces)
     def _(i):
-        rows = pl.ds(pl.multiple_of(i * chunk, chunk), chunk)
+        rows = piece(i)
         near_copy(i).wait_recv()
         near_t[:, rows] += (
             near_before * before_t[:, rows] + near_after * near_recv[i].astype(f32)
@@ -337,7 +483,7 @@
         couple[2][1] * ret2_recv[0].astype(f32) + couple[2][0] * ret2_recv[1].astype(f32)
     ) / rank
     down = far1 + dot_nt(down, transfer_in[1, child2], highest)
-    down = far0 + dot_nt(down, transfer_in[0, child1], highest)
+    down = far0 + dot_nt(down, transfer_in[0, quarter], highest)
     down_high = down.astype(bf16)
     down_low = (down - down_high.astype(f32)).astype(bf16)
     far = dot_nt(down_high, leaf[...]) + dot_nt(down_low, leaf[...])
@@ -345,10 +491,14 @@
     width = labels_in.shape[1]
     out_ref[...] = (total[:width] / total[width : width + 1]).T
 
-    for copy in [c_up8, c_down8, c_up2, c_down2, c_down1, c_labels, c_w0, c_w1, c_w2, c_ret0]:
+    sent = [c_up8, c_down8, c_down, c_down1, c_labels, c_w0, c_w1, c_shift2, c_ret0, c_ret1]
+    for copy in sent + c_t1 + c_share1 + c_t2 + c_share2 + c_share_next + c_ret2:
         copy.wait_send()
-    for copy in c_t1 + c_t2 + c_ret1 + c_ret2:
-        copy.wait_send()
+
+    @pl.when(even)
+    def _():
+        up2_copy().wait_send()
+        ret1_down_copy().wait_send()
 
     @pl.loop(0, pieces)
     def _(i):
@@ -365,14 +515,24 @@
         rank = skeleton.shape[0]
         pieces = count // chunk
         node = lambda *lead: pltpu.VMEM((*lead, aug, rank), bf16)
-        vmem = pl.BlockSpec(memory_space=pltpu.VMEM)
-        smem = pl.BlockSpec(memory_space=pltpu.SMEM)
+        parts = lambda lead: pltpu.VMEM((lead, part, rank), bf16)
+        anywhere = pl.BlockSpec(memory_space=pl.ANY)
+        couple_peer = couple_peer.transpose(0, 2, 1)
+        couple_live = couple_live.transpose(0, 2, 1)
         return pl.pallas_call(
             functools.partial(kernel, n),
             out_shape=jax.ShapeDtypeStruct((count, width), f32),
-            in_specs=[vmem] * 4 + [smem] * 4,
-            out_specs=vmem,
+            in_specs=[anywhere] * 8,
+            out_specs=pl.BlockSpec(memory_space=pltpu.VMEM),
             scratch_shapes=[
+                pltpu.VMEM((count, depth), bf16),
+                pltpu.VMEM((count, width), bf16),
+                pltpu.VMEM((rank, depth), bf16),
+                pltpu.VMEM(transfer.shape, f32),
+                pltpu.SMEM(near_peer.shape, jnp.int32),
+                pltpu.SMEM(near_live.shape, jnp.int32),
+                pltpu.SMEM(couple_peer.shape, jnp.int32),
+                pltpu.SMEM(couple_live.shape, jnp.int32),
                 pltpu.VMEM((count, depth), bf16),
                 pltpu.VMEM((count, 1), f32),
                 pltpu.VMEM((1, count), f32),
@@ -389,14 +549,16 @@
                 pltpu.VMEM((aug, count), f32),
                 node(),
                 node(),
-                node(),
-                node(3),
-                node(),
-                node(3),
-                node(),
-                node(),
-                node(),
-                node(),
+                pltpu.VMEM((aug, rank), f32),
+                node(),
+                parts(3),
+                parts(4),
+                node(),
+                node(),
+                pltpu.VMEM((part, rank), bf16),
+                parts(3),
+                parts(4),
+                parts(4),
                 node(),
                 node(),
                 node(2),
@@ -405,11 +567,12 @@
                 node(2),
                 node(pieces),
                 node(pieces),
+                pltpu.SemaphoreType.DMA((INPUTS,)),
                 pltpu.SemaphoreType.DMA((FLOWS,)),
                 pltpu.SemaphoreType.DMA((FLOWS,)),
             ],
             compiler_params=pltpu.CompilerParams(
-                collective_id=0, has_side_effects=True, vmem_limit_bytes=48 * 2**20
+                collective_id=0, has_side_effects=True, vmem_limit_bytes=60 * 2**20
             ),
         )(documents, labels, skeleton, transfer, near_peer, near_live, couple_peer, couple_live)
 

time: 136 us -> 120 us (0.88)
  the two profiles are of different devices: /device:TPU:32 before, /device:TPU:33 now
where the time goes in v2:
time: 120 us
  Pallas kernels  118 us (98%)
  local copies, waits for them, and re-layouts  1.77 us (1%)
    pallas_call x1, Pallas kernels, local(): pl.pallas_call(functools.partial(kernel, n), out_shape=jax.ShapeDtypeStru...  118 us

profile of v2, /device:TPU:33, one launch (start us, length us, event | category | flops | bytes accessed | tf_op | source)
XLA Modules:
  0.0 120.0 jit_solution(16120250541963933382)
XLA Ops:
  0.0 118.2 %shard_map.82 = f32[768,128]{1,0:T(8,128)} custom-call(bf16[768,1024]{1,0:T(8,128)(2,1)} %docs_hbm.1, bf16[768,128]{1,0:T(8,128)(2,1)} %labels_hbm.1, bf16[256,1024]{1,0:T(8,128)(2,1)} %skel_hbm.1, f32[2,4,256,256]{3,2,1,0:T(8,128)} %transfer_hbm.1, s32[1,2]{1,0:T(1,128)} %near_peer_hbm.1, s32[1,2]{1,0:T(1,128)} %near_live_hbm.1, s32[1,2,3]{2,1,0:T(2,128)} %bitcast.2, ...), custom_call_target="tpu_custom_call" | custom-call | tf_op jit(solution)/shard_map/pallas_call | solution.py:522
  118.3 1.8 %copy.10 = f32[768,128]{1,0:T(8,128)} copy(f32[768,128]{1,0:T(8,128)} %shard_map.82) | data formatting | bytes 786432

commit v3 on v2

--- a/solution.py
+++ b/solution.py
@@ -17,7 +17,7 @@
 chunk = 256
 aug = 144
 
-PTS_UP8, PTS_DOWN8, PTS_UP2, PTS_DOWN, PTS_DOWN1 = range(5)
+PTS_UP2, PTS_DOWN, PTS_DOWN1 = range(3)
 DOCS = 5
 LABELS = 8
 W0 = 9
@@ -31,7 +31,10 @@
 RET0 = 27
 RET1_DOWN, RET1_UP, RET2_DOWN, RET2_UP = 28, 29, 30, 31
 NEAR = 32
-FLOWS = 35
+PTS_UP8, PTS_DOWN8 = 35, 39
+FLOWS = 43
+
+strips = 4
 
 part = 48
 step_rows = 32
@@ -224,8 +227,23 @@
     pts[...] = normalize(skel_in[...])
     pl.semaphore_wait(barrier, len(greeted))
 
-    c_up8 = send(PTS_UP8, pts, p8.at[0], at(8))
-    c_down8 = send(PTS_DOWN8, pts, p8.at[1], at(-8))
+    def strip_copy(slot, k):
+        size = rank // strips
+        rows = pl.ds(k * size, size)
+        return pltpu.make_async_remote_copy(
+            src_ref=pts.at[rows],
+            dst_ref=p8.at[slot, rows],
+            send_sem=send_sem.at[(PTS_UP8, PTS_DOWN8)[slot] + k],
+            recv_sem=recv_sem.at[(PTS_UP8, PTS_DOWN8)[slot] + k],
+            device_id=(at((8, -8)[slot]),),
+            device_id_type=MESH,
+        )
+
+    def strip(k):
+        strip_copy(0, k).start()
+        strip_copy(1, k).start()
+
+    strip(0)
 
     def up2_copy():
         return pltpu.make_async_remote_copy(
@@ -247,14 +265,6 @@
             device_id_type=MESH,
         )
 
-    c_down = send(PTS_DOWN, pts, p2.at[1], jnp.where(even, at(-2), at(-4)))
-
-    @pl.when(even)
-    def _():
-        up2_copy().start()
-
-    c_down1 = send(PTS_DOWN1, pts, p1, at(-1))
-
     def docs_copy(i):
         return pltpu.make_async_remote_copy(
             src_ref=docs.at[piece(i)],
@@ -279,10 +289,8 @@
     def _(i):
         docs_fetch(i).wait()
         docs[piece(i), :] = normalize(docs_in[piece(i), :])
-        docs_copy(i).start()
 
     f_labels.wait()
-    c_labels = send(LABELS, labels_in, labels_r, at(1))
     lab_t[...] = augmented(labels_in[...])
     pts_bias = bias_of(pts[...])
     pts_row = as_row(pts_bias)
@@ -298,7 +306,6 @@
 
     w0 = dot_nn(lab_t[...], leaf[...]) * (1.0 / count)
     w0_send[...] = w0.astype(bf16)
-    c_w0 = send(W0, w0_send, w0_recv, at(-1))
 
     f_transfer.wait()
     child2 = lax.rem(me // 4, 4)
@@ -315,6 +322,9 @@
         for j in range(3)
     ]
 
+    c_w0 = send(W0, w0_send, w0_recv, at(-1))
+    strip(1)
+
     near_t[...] = jnp.zeros_like(near_t)
 
     @pl.loop(0, pieces)
@@ -332,20 +342,14 @@
         t1_recv[1].astype(f32) + t1_recv[2].astype(f32)
     )
     w1_parts[quarter] = w1.astype(bf16)
+    t2 = 0.25 * dot_nn(w1, transfer_in[1, child2], highest)
+    t2_send[...] = t2.astype(bf16)
+    c_t2 = [send(T2 + j, t2_send, t2_recv.at[j], sibling(j + 1, 4)) for j in range(3)]
     c_share1 = [
         send(SHARE1 + j, w1_parts.at[quarter], w1_parts.at[quarter], sibling(j + 1, 1))
         for j in range(3)
     ]
-    t2 = 0.25 * dot_nn(w1, transfer_in[1, child2], highest)
-    t2_send[...] = t2.astype(bf16)
-    c_t2 = [send(T2 + j, t2_send, t2_recv.at[j], sibling(j + 1, 4)) for j in range(3)]
-
-    c_down1.wait_recv()
-    c_w0.wait_recv()
-    pair = kernel_tile(pts[...], pts_bias, p1[...], as_row(bias_of(p1[...]))).astype(bf16)
-    ret0_send[...] = dot_nn(w0_send[...], pair).astype(bf16)
-    c_ret0 = send(RET0, ret0_send, ret0_recv, at(1))
-    after0 = dot_nt(w0_recv[...], pair)
+    strip(2)
 
     for copy in c_t2:
         copy.wait_recv()
@@ -361,12 +365,53 @@
         copy.wait_recv()
     w1_own[...] = whole(w1_parts)
     c_w1 = send(W1, w1_own, w1_next, next1)
+    strip(3)
 
     c_shift2.wait_recv()
     c_share_next = [
         send(SHARE_NEXT + j, w2_next.at[quarter], w2_next.at[quarter], sibling(j + 1, 1))
         for j in range(3)
     ]
+
+    c_down1 = send(PTS_DOWN1, pts, p1, at(-1))
+    c_down = send(PTS_DOWN, pts, p2.at[1], jnp.where(even, at(-2), at(-4)))
+
+    @pl.when(even)
+    def _():
+        up2_copy().start()
+
+    c_labels = send(LABELS, labels_in, labels_r, at(1))
+    docs_copy(0).start()
+
+    for copy in c_share2 + c_share_next:
+        copy.wait_recv()
+    own2 = whole(w2_parts)
+    other2 = whole(w2_next)
+    w_before = jnp.where(low2, other2, own2)
+    w_after = jnp.where(low2, own2, other2)
+    for k in range(strips):
+        strip_copy(0, k).wait_recv()
+        strip_copy(1, k).wait_recv()
+    pair = kernel_tile(
+        p8[0], bias_of(p8[0]), p8[1], as_row(bias_of(p8[1]))
+    ).astype(bf16)
+    ret2_send[0] = dot_nt(w_after, pair).astype(bf16)
+    ret2_send[1] = dot_nn(w_before, pair).astype(bf16)
+    c_ret2 = [
+        send(RET2_DOWN, ret2_send.at[0], ret2_recv.at[0], at(-8)),
+        send(RET2_UP, ret2_send.at[1], ret2_recv.at[1], at(8)),
+    ]
+
+    @pl.loop(1, pieces)
+    def _(i):
+        docs_copy(i).start()
+
+    c_down1.wait_recv()
+    c_w0.wait_recv()
+    pair = kernel_tile(pts[...], pts_bias, p1[...], as_row(bias_of(p1[...]))).astype(bf16)
+    ret0_send[...] = dot_nn(w0_send[...], pair).astype(bf16)
+    c_ret0 = send(RET0, ret0_send, ret0_recv, at(1))
+    after0 = dot_nt(w0_recv[...], pair)
 
     c_down.wait_recv()
 
@@ -412,24 +457,6 @@
         near_copy(i).start()
         before_t[...] += dot_nn(lab_tr[:, rows], tile)
 
-    for copy in c_share2 + c_share_next:
-        copy.wait_recv()
-    own2 = whole(w2_parts)
-    other2 = whole(w2_next)
-    w_before = jnp.where(low2, other2, own2)
-    w_after = jnp.where(low2, own2, other2)
-    c_up8.wait_recv()
-    c_down8.wait_recv()
-    pair = kernel_tile(
-        p8[0], bias_of(p8[0]), p8[1], as_row(bias_of(p8[1]))
-    ).astype(bf16)
-    ret2_send[0] = dot_nt(w_after, pair).astype(bf16)
-    ret2_send[1] = dot_nn(w_before, pair).astype(bf16)
-    c_ret2 = [
-        send(RET2_DOWN, ret2_send.at[0], ret2_recv.at[0], at(-8)),
-        send(RET2_UP, ret2_send.at[1], ret2_recv.at[1], at(8)),
-    ]
-
     def tally(peer, live, code, inside):
         total = jnp.int32(0)
         for p, v in zip(peer, live):
@@ -468,14 +495,6 @@
     far1 = (
         couple[1][1] * ret1_recv[0].astype(f32) + couple[1][0] * ret1_recv[1].astype(f32)
     ) / rank
-
-    @pl.loop(0, pieces)
-    def _(i):
-        rows = piece(i)
-        near_copy(i).wait_recv()
-        near_t[:, rows] += (
-            near_before * before_t[:, rows] + near_after * near_recv[i].astype(f32)
-        )
 
     for copy in c_ret2:
         copy.wait_recv()
@@ -487,13 +506,26 @@
     down_high = down.astype(bf16)
     down_low = (down - down_high.astype(f32)).astype(bf16)
     far = dot_nt(down_high, leaf[...]) + dot_nt(down_low, leaf[...])
+
+    @pl.loop(0, pieces)
+    def _(i):
+        rows = piece(i)
+        near_copy(i).wait_recv()
+        near_t[:, rows] += (
+            near_before * before_t[:, rows] + near_after * near_recv[i].astype(f32)
+        )
+
     total = near_t[...] + (far_gain / rank) * far
     width = labels_in.shape[1]
     out_ref[...] = (total[:width] / total[width : width + 1]).T
 
-    sent = [c_up8, c_down8, c_down, c_down1, c_labels, c_w0, c_w1, c_shift2, c_ret0, c_ret1]
+    sent = [c_down, c_down1, c_labels, c_w0, c_w1, c_shift2, c_ret0, c_ret1]
     for copy in sent + c_t1 + c_share1 + c_t2 + c_share2 + c_share_next + c_ret2:
         copy.wait_send()
+
+    for k in range(strips):
+        strip_copy(0, k).wait_send()
+        strip_copy(1, k).wait_send()
 
     @pl.when(even)
     def _():

time: 120 us -> 111 us (0.925)
  the two profiles are of different devices: /device:TPU:33 before, /device:TPU:1 now
where the time goes in v3:
time: 111 us
  Pallas kernels  109 us (98%)
  local copies, waits for them, and re-layouts  1.77 us (2%)
    pallas_call x1, Pallas kernels, local(): pl.pallas_call(functools.partial(kernel, n), out_shape=jax.ShapeDtypeStru...  109 us

profile of v3, /device:TPU:1, one launch (start us, length us, event | category | flops | bytes accessed | tf_op | source)
XLA Modules:
  0.0 111.3 jit_solution(9335379610230566836)
XLA Ops:
  0.0 109.5 %shard_map.82 = f32[768,128]{1,0:T(8,128)} custom-call(bf16[768,1024]{1,0:T(8,128)(2,1)} %docs_hbm.1, bf16[768,128]{1,0:T(8,128)(2,1)} %labels_hbm.1, bf16[256,1024]{1,0:T(8,128)(2,1)} %skel_hbm.1, f32[2,4,256,256]{3,2,1,0:T(8,128)} %transfer_hbm.1, s32[1,2]{1,0:T(1,128)} %near_peer_hbm.1, s32[1,2]{1,0:T(1,128)} %near_live_hbm.1, s32[1,2,3]{2,1,0:T(2,128)} %bitcast.2, ...), custom_call_target="tpu_custom_call" | custom-call | tf_op jit(solution)/shard_map/pallas_call | solution.py:554
  109.5 1.8 %copy.10 = f32[768,128]{1,0:T(8,128)} copy(f32[768,128]{1,0:T(8,128)} %shard_map.82) | data formatting | bytes 786432

commit v4 on v3

--- a/solution.py
+++ b/solution.py
@@ -29,12 +29,14 @@
 SHIFT2 = 23
 SHARE_NEXT = 24
 RET0 = 27
-RET1_DOWN, RET1_UP, RET2_DOWN, RET2_UP = 28, 29, 30, 31
-NEAR = 32
-PTS_UP8, PTS_DOWN8 = 35, 39
+RET1_DOWN, RET1_UP = 28, 29
+NEAR = 30
+PTS8 = 33
+FORWARD, W_FORWARD = 37, 38
+RET2 = 39
 FLOWS = 43
 
-strips = 4
+strips = 2
 
 part = 48
 step_rows = 32
@@ -139,6 +141,7 @@
     t2_recv,
     w2_parts,
     w2_next,
+    w2_pair,
     ret0_send,
     ret0_recv,
     ret1_send,
@@ -198,92 +201,150 @@
     def sibling(bits, unit):
         return me + flipped(me // unit, bits) * unit
 
-    def send(flow, src, dst, target):
-        copy = pltpu.make_async_remote_copy(
-            src_ref=src,
-            dst_ref=dst,
-            send_sem=send_sem.at[flow],
-            recv_sem=recv_sem.at[flow],
-            device_id=(target,),
-            device_id_type=MESH,
+    def inside(offset):
+        return jnp.logical_and(me + offset >= 0, me + offset < n)
+
+    class Flow:
+        def __init__(self, flow, src, dst, target, out=None, into=None):
+            self.copy = pltpu.make_async_remote_copy(
+                src_ref=src,
+                dst_ref=dst,
+                send_sem=send_sem.at[flow],
+                recv_sem=recv_sem.at[flow],
+                device_id=(target,),
+                device_id_type=MESH,
+            )
+            self.out = out
+            self.into = into
+
+        def start(self):
+            when(self.out, self.copy.start)
+            return self
+
+        def wait_recv(self):
+            when(self.into, self.copy.wait_recv)
+
+        def wait_send(self):
+            when(self.out, self.copy.wait_send)
+
+    def when(condition, action):
+        if condition is None:
+            action()
+        else:
+            pl.when(condition)(lambda: action() and None)
+
+    def along(flow, src, dst, offset, out=True, into=True):
+        return Flow(
+            flow,
+            src,
+            dst,
+            at(offset),
+            inside(offset) if out is True else jnp.logical_and(inside(offset), out),
+            inside(-offset) if into is True else jnp.logical_and(inside(-offset), into),
         )
-        copy.start()
-        return copy
+
+    def send(flow, src, dst, target, out=None, into=None):
+        return Flow(flow, src, dst, target, out, into).start()
 
     even = core == 0
     odd = core == 1
     next1 = jnp.where(even, jnp.where(quarter < 2, at(-2), at(2)), at(-4))
     low1 = jnp.logical_and(even, quarter < 2)
-    low2 = lax.rem(me, 16) < 8
-    next2 = jnp.where(low2, at(-8), at(8))
+
+    out1 = jnp.where(even, jnp.where(quarter < 2, me >= 2, me + 2 < n), me >= 4)
+    into1 = jnp.where(even, out1, me + 4 < n)
+
+    spot = lax.rem(me // 2, 16)
+    base = me - lax.rem(me, 32)
+    up4 = base + lax.rem(spot + 4, 16) * 2 + core
+    down4 = base + lax.rem(spot + 12, 16) * 2 + core
+    half = spot // 8
+    central = jnp.logical_and(spot >= 4, spot < 12)
+    meet = central == even
+    first_half = half == 0
+    meeting = jnp.where(first_half == even, up4, down4)
+    from_a = jnp.where(even, down4, up4)
+    from_b = jnp.where(even, up4, down4)
+    other_half = jnp.where(central == first_half, up4, down4)
+    has_next = me < n - 32
+    has_last = me >= 32
+    meet_next = jnp.logical_and(meet, has_next)
+    meet_last = jnp.logical_and(meet, has_last)
+    b_next = jnp.logical_and(half == 1, has_next)
+    a_last = jnp.logical_and(first_half, has_last)
 
     barrier = pltpu.get_barrier_semaphore()
-    greeted = [at(1), at(-1), at(2), at(-2), at(4), at(-4), at(8), at(-8)]
-    greeted += [sibling(3, 1), sibling(3, 4)]
-    for other in greeted:
+    reach = (1, 2, 4, 32)
+    for other in [sibling(3, 1), sibling(3, 4), up4, down4]:
         pl.semaphore_signal(barrier, inc=1, device_id=(other,), device_id_type=MESH)
+    for offset in [sign * far for far in reach for sign in (1, -1)]:
+
+        @pl.when(inside(offset))
+        def _(offset=offset):
+            pl.semaphore_signal(barrier, inc=1, device_id=(at(offset),), device_id_type=MESH)
+
+    @pl.when(b_next)
+    def _():
+        pl.semaphore_signal(barrier, inc=1, device_id=(meeting + 32,), device_id_type=MESH)
+
+    @pl.when(jnp.logical_and(first_half, jnp.logical_not(has_last)))
+    def _():
+        ret2_recv[1] = jnp.zeros_like(ret2_recv[1])
+
+    @pl.when(jnp.logical_and(half == 1, jnp.logical_not(has_next)))
+    def _():
+        ret2_recv[0] = jnp.zeros_like(ret2_recv[0])
+
+    @pl.when(me < 4)
+    def _():
+        p2[0] = jnp.zeros_like(p2[0])
+        ret1_recv[1] = jnp.zeros_like(ret1_recv[1])
+
+    @pl.when(me >= n - 4)
+    def _():
+        p2[1] = jnp.zeros_like(p2[1])
+        ret1_recv[0] = jnp.zeros_like(ret1_recv[0])
+
+    @pl.when(jnp.logical_not(into1))
+    def _():
+        w1_next[...] = jnp.zeros_like(w1_next)
+
+    @pl.when(me == 0)
+    def _():
+        docs_r[...] = jnp.zeros_like(docs_r)
+        labels_r[...] = jnp.zeros_like(labels_r)
+        ret0_recv[...] = jnp.zeros_like(ret0_recv)
+
+    @pl.when(me == n - 1)
+    def _():
+        p1[...] = jnp.zeros_like(p1)
+        w0_recv[...] = jnp.zeros_like(w0_recv)
+        near_recv[...] = jnp.zeros_like(near_recv)
 
     f_skel.wait()
     pts[...] = normalize(skel_in[...])
-    pl.semaphore_wait(barrier, len(greeted))
+    greetings = 4 + jnp.where(meet_last, 1, 0)
+    for offset in [sign * far for far in reach for sign in (1, -1)]:
+        greetings = greetings + jnp.where(inside(offset), 1, 0)
+    pl.semaphore_wait(barrier, greetings)
 
     def strip_copy(slot, k):
         size = rank // strips
         rows = pl.ds(k * size, size)
-        return pltpu.make_async_remote_copy(
-            src_ref=pts.at[rows],
-            dst_ref=p8.at[slot, rows],
-            send_sem=send_sem.at[(PTS_UP8, PTS_DOWN8)[slot] + k],
-            recv_sem=recv_sem.at[(PTS_UP8, PTS_DOWN8)[slot] + k],
-            device_id=(at((8, -8)[slot]),),
-            device_id_type=MESH,
+        return Flow(
+            PTS8 + slot * strips + k, pts.at[rows], p8.at[slot, rows], meeting, None, meet
         )
 
     def strip(k):
-        strip_copy(0, k).start()
-        strip_copy(1, k).start()
+        strip_copy(half, k).start()
 
     strip(0)
 
-    def up2_copy():
-        return pltpu.make_async_remote_copy(
-            src_ref=pts,
-            dst_ref=p2.at[0],
-            send_sem=send_sem.at[PTS_UP2],
-            recv_sem=recv_sem.at[PTS_UP2],
-            device_id=(at(2),),
-            device_id_type=MESH,
-        )
-
-    def ret1_down_copy():
-        return pltpu.make_async_remote_copy(
-            src_ref=ret1_send.at[0],
-            dst_ref=ret1_recv.at[0],
-            send_sem=send_sem.at[RET1_DOWN],
-            recv_sem=recv_sem.at[RET1_DOWN],
-            device_id=(at(-2),),
-            device_id_type=MESH,
-        )
-
     def docs_copy(i):
-        return pltpu.make_async_remote_copy(
-            src_ref=docs.at[piece(i)],
-            dst_ref=docs_r.at[piece(i)],
-            send_sem=send_sem.at[DOCS + i],
-            recv_sem=recv_sem.at[DOCS + i],
-            device_id=(at(1),),
-            device_id_type=MESH,
-        )
+        return along(DOCS + i, docs.at[piece(i)], docs_r.at[piece(i)], 1)
 
     def near_copy(i):
-        return pltpu.make_async_remote_copy(
-            src_ref=near_send.at[i],
-            dst_ref=near_recv.at[i],
-            send_sem=send_sem.at[NEAR + i],
-            recv_sem=recv_sem.at[NEAR + i],
-            device_id=(at(-1),),
-            device_id_type=MESH,
-        )
+        return along(NEAR + i, near_send.at[i], near_recv.at[i], -1)
 
     @pl.loop(0, pieces)
     def _(i):
@@ -322,7 +383,7 @@
         for j in range(3)
     ]
 
-    c_w0 = send(W0, w0_send, w0_recv, at(-1))
+    c_w0 = along(W0, w0_send, w0_recv, -1).start()
     strip(1)
 
     near_t[...] = jnp.zeros_like(near_t)
@@ -349,57 +410,100 @@
         send(SHARE1 + j, w1_parts.at[quarter], w1_parts.at[quarter], sibling(j + 1, 1))
         for j in range(3)
     ]
-    strip(2)
+    level1 = [
+        along(PTS_DOWN, pts, p2.at[1], -2, even, even),
+        along(PTS_DOWN, pts, p2.at[1], -4, odd, odd),
+        along(PTS_UP2, pts, p2.at[0], 2, even, even),
+    ]
+    for copy in level1:
+        copy.start()
 
     for copy in c_t2:
         copy.wait_recv()
     w2 = (t2 + t2_recv[0].astype(f32)) + (t2_recv[1].astype(f32) + t2_recv[2].astype(f32))
     w2_parts[quarter] = w2.astype(bf16)
-    c_shift2 = send(SHIFT2, w2_parts.at[quarter], w2_next.at[quarter], next2)
+    c_shift2 = send(SHIFT2, w2_parts.at[quarter], w2_next.at[quarter], other_half)
     c_share2 = [
-        send(SHARE2 + j, w2_parts.at[quarter], w2_parts.at[quarter], sibling(j + 1, 1))
+        send(
+            SHARE2 + j,
+            w2_parts.at[quarter],
+            w2_parts.at[quarter],
+            sibling(j + 1, 1),
+            meet if j == 1 else jnp.logical_not(meet),
+            meet,
+        )
         for j in range(3)
     ]
 
     for copy in c_share1:
         copy.wait_recv()
     w1_own[...] = whole(w1_parts)
-    c_w1 = send(W1, w1_own, w1_next, next1)
-    strip(3)
+    c_w1 = send(W1, w1_own, w1_next, next1, out1, into1)
+    for k in range(strips):
+        strip_copy(1, k).wait_recv()
+    c_forward = send(FORWARD, p8.at[1], p8.at[2], at(32), meet_next, meet_last)
+    c_down1 = along(PTS_DOWN1, pts, p1, -1).start()
+    c_labels = along(LABELS, labels_in, labels_r, 1).start()
 
     c_shift2.wait_recv()
     c_share_next = [
-        send(SHARE_NEXT + j, w2_next.at[quarter], w2_next.at[quarter], sibling(j + 1, 1))
+        send(
+            SHARE_NEXT + j,
+            w2_next.at[quarter],
+            w2_next.at[quarter],
+            sibling(j + 1, 1),
+            meet if j == 1 else jnp.logical_not(meet),
+            meet,
+        )
         for j in range(3)
     ]
 
-    c_down1 = send(PTS_DOWN1, pts, p1, at(-1))
-    c_down = send(PTS_DOWN, pts, p2.at[1], jnp.where(even, at(-2), at(-4)))
-
-    @pl.when(even)
-    def _():
-        up2_copy().start()
-
-    c_labels = send(LABELS, labels_in, labels_r, at(1))
     docs_copy(0).start()
 
     for copy in c_share2 + c_share_next:
         copy.wait_recv()
-    own2 = whole(w2_parts)
-    other2 = whole(w2_next)
-    w_before = jnp.where(low2, other2, own2)
-    w_after = jnp.where(low2, own2, other2)
+
+    @pl.when(meet)
+    def _():
+        own2 = whole(w2_parts)
+        other2 = whole(w2_next)
+        w2_pair[0] = jnp.where(first_half, own2, other2)
+        w2_pair[1] = jnp.where(first_half, other2, own2)
+
+    c_wforward = send(W_FORWARD, w2_pair.at[1], w2_pair.at[2], at(32), meet_next, meet_last)
     for k in range(strips):
         strip_copy(0, k).wait_recv()
-        strip_copy(1, k).wait_recv()
-    pair = kernel_tile(
-        p8[0], bias_of(p8[0]), p8[1], as_row(bias_of(p8[1]))
-    ).astype(bf16)
-    ret2_send[0] = dot_nt(w_after, pair).astype(bf16)
-    ret2_send[1] = dot_nn(w_before, pair).astype(bf16)
+
+    def couple2(left, right):
+        return kernel_tile(
+            left, bias_of(left), right, as_row(bias_of(right))
+        ).astype(bf16)
+
+    @pl.when(meet)
+    def _():
+        pair = couple2(p8[0], p8[1])
+        ret2_send[0] = dot_nt(w2_pair[1], pair).astype(bf16)
+        ret2_send[1] = dot_nn(w2_pair[0], pair).astype(bf16)
+
+    def ret2(j, slot, target, out, into):
+        return send(RET2 + j, ret2_send.at[j], ret2_recv.at[slot], target, out, into)
+
     c_ret2 = [
-        send(RET2_DOWN, ret2_send.at[0], ret2_recv.at[0], at(-8)),
-        send(RET2_UP, ret2_send.at[1], ret2_recv.at[1], at(8)),
+        ret2(0, 0, from_a, meet, first_half),
+        ret2(1, 1, from_b, meet, half == 1),
+    ]
+    c_forward.wait_recv()
+    c_wforward.wait_recv()
+
+    @pl.when(meet_last)
+    def _():
+        pair = couple2(p8[2], p8[0])
+        ret2_send[2] = dot_nt(w2_pair[0], pair).astype(bf16)
+        ret2_send[3] = dot_nn(w2_pair[2], pair).astype(bf16)
+
+    c_ret2 += [
+        ret2(2, 0, from_b - 32, meet_last, b_next),
+        ret2(3, 1, from_a, meet_last, a_last),
     ]
 
     @pl.loop(1, pieces)
@@ -410,14 +514,11 @@
     c_w0.wait_recv()
     pair = kernel_tile(pts[...], pts_bias, p1[...], as_row(bias_of(p1[...]))).astype(bf16)
     ret0_send[...] = dot_nn(w0_send[...], pair).astype(bf16)
-    c_ret0 = send(RET0, ret0_send, ret0_recv, at(1))
+    c_ret0 = along(RET0, ret0_send, ret0_recv, 1).start()
     after0 = dot_nt(w0_recv[...], pair)
 
-    c_down.wait_recv()
-
-    @pl.when(even)
-    def _():
-        up2_copy().wait_recv()
+    for copy in level1:
+        copy.wait_recv()
 
     @pl.when(odd)
     def _():
@@ -431,13 +532,11 @@
     w_after = jnp.where(low1, w1_own[...], w1_next[...])
     ret1_send[0] = dot_nt(w_after, pair).astype(bf16)
     ret1_send[1] = dot_nn(w_before, pair).astype(bf16)
-    c_ret1 = send(
-        RET1_UP, ret1_send.at[1], ret1_recv.at[1], jnp.where(even, at(2), at(4))
-    )
-
-    @pl.when(even)
-    def _():
-        ret1_down_copy().start()
+    c_ret1 = [
+        along(RET1_UP, ret1_send.at[1], ret1_recv.at[1], 2, even, even).start(),
+        along(RET1_UP, ret1_send.at[1], ret1_recv.at[1], 4, odd, odd).start(),
+        along(RET1_DOWN, ret1_send.at[0], ret1_recv.at[0], -2, even, even).start(),
+    ]
 
     @pl.when(odd)
     def _():
@@ -486,11 +585,8 @@
 
     c_ret0.wait_recv()
     far0 = (couple[0][0] * ret0_recv[...].astype(f32) + couple[0][1] * after0) / rank
-    c_ret1.wait_recv()
-
-    @pl.when(even)
-    def _():
-        ret1_down_copy().wait_recv()
+    for copy in c_ret1:
+        copy.wait_recv()
 
     far1 = (
         couple[1][1] * ret1_recv[0].astype(f32) + couple[1][0] * ret1_recv[1].astype(f32)
@@ -519,18 +615,14 @@
     width = labels_in.shape[1]
     out_ref[...] = (total[:width] / total[width : width + 1]).T
 
-    sent = [c_down, c_down1, c_labels, c_w0, c_w1, c_shift2, c_ret0, c_ret1]
-    for copy in sent + c_t1 + c_share1 + c_t2 + c_share2 + c_share_next + c_ret2:
-        copy.wait_send()
-
-    for k in range(strips):
-        strip_copy(0, k).wait_send()
-        strip_copy(1, k).wait_send()
-
-    @pl.when(even)
-    def _():
-        up2_copy().wait_send()
-        ret1_down_copy().wait_send()
+    for copies in (
+        [c_down1, c_labels, c_w0, c_w1, c_shift2, c_ret0],
+        c_t1 + c_share1 + c_t2 + c_share2 + c_share_next,
+        level1 + c_ret1 + c_ret2,
+        [c_forward, c_wforward] + [strip_copy(half, k) for k in range(strips)],
+    ):
+        for copy in copies:
+            copy.wait_send()
 
     @pl.loop(0, pieces)
     def _(i):
@@ -574,7 +666,7 @@
                 pltpu.VMEM((count, depth), bf16),
                 pltpu.VMEM((count, width), bf16),
                 pltpu.VMEM((aug, count), bf16),
-                pltpu.VMEM((2, rank, depth), bf16),
+                pltpu.VMEM((3, rank, depth), bf16),
                 pltpu.VMEM((2, rank, depth), bf16),
                 pltpu.VMEM((rank, depth), bf16),
                 pltpu.VMEM((aug, count), f32),
@@ -591,11 +683,12 @@
                 parts(3),
                 parts(4),
                 parts(4),
+                node(3),
                 node(),
                 node(),
                 node(2),
                 node(2),
-                node(2),
+                node(4),
                 node(2),
                 node(pieces),
                 node(pieces),

time: 111 us -> 102 us (0.919)
  the two profiles are of different devices: /device:TPU:1 before, /device:TPU:25 now
where the time goes in v4:
time: 102 us
  Pallas kernels  99.9 us (98%)
  local copies, waits for them, and re-layouts  1.77 us (2%)
    pallas_call x1, Pallas kernels, local(): pl.pallas_call(functools.partial(kernel, n), out_shape=jax.ShapeDtypeStru...  99.9 us

profile of v4, /device:TPU:25, one launch (start us, length us, event | category | flops | bytes accessed | tf_op | source)
XLA Modules:
  0.0 101.7 jit_solution(12821247313535917621)
XLA Ops:
  0.0 99.9 %shard_map.82 = f32[768,128]{1,0:T(8,128)} custom-call(bf16[768,1024]{1,0:T(8,128)(2,1)} %docs_hbm.1, bf16[768,128]{1,0:T(8,128)(2,1)} %labels_hbm.1, bf16[256,1024]{1,0:T(8,128)(2,1)} %skel_hbm.1, f32[2,4,256,256]{3,2,1,0:T(8,128)} %transfer_hbm.1, s32[1,2]{1,0:T(1,128)} %near_peer_hbm.1, s32[1,2]{1,0:T(1,128)} %near_live_hbm.1, s32[1,2,3]{2,1,0:T(2,128)} %bitcast.2, ...), custom_call_target="tpu_custom_call" | custom-call | tf_op jit(solution)/shard_map/pallas_call | solution.py:646
  99.9 1.8 %copy.10 = f32[768,128]{1,0:T(8,128)} copy(f32[768,128]{1,0:T(8,128)} %shard_map.82) | data formatting | bytes 786432

commit v5 on v4

--- a/solution.py
+++ b/solution.py
@@ -323,11 +323,6 @@
 
     f_skel.wait()
     pts[...] = normalize(skel_in[...])
-    greetings = 4 + jnp.where(meet_last, 1, 0)
-    for offset in [sign * far for far in reach for sign in (1, -1)]:
-        greetings = greetings + jnp.where(inside(offset), 1, 0)
-    pl.semaphore_wait(barrier, greetings)
-
     def strip_copy(slot, k):
         size = rank // strips
         rows = pl.ds(k * size, size)
@@ -338,7 +333,6 @@
     def strip(k):
         strip_copy(half, k).start()
 
-    strip(0)
 
     def docs_copy(i):
         return along(DOCS + i, docs.at[piece(i)], docs_r.at[piece(i)], 1)
@@ -373,6 +367,12 @@
     t1 = 0.25 * dot_nn(w0, transfer_in[0, quarter], highest)
     t1_sum[...] = t1
     t1_send[...] = t1.astype(bf16)
+
+    greetings = 4 + jnp.where(meet_last, 1, 0)
+    for offset in [sign * far for far in reach for sign in (1, -1)]:
+        greetings = greetings + jnp.where(inside(offset), 1, 0)
+    pl.semaphore_wait(barrier, greetings)
+
     c_t1 = [
         send(
             T1 + j,
@@ -384,7 +384,8 @@
     ]
 
     c_w0 = along(W0, w0_send, w0_recv, -1).start()
-    strip(1)
+
+    strip(0)
 
     near_t[...] = jnp.zeros_like(near_t)
 
@@ -410,13 +411,7 @@
         send(SHARE1 + j, w1_parts.at[quarter], w1_parts.at[quarter], sibling(j + 1, 1))
         for j in range(3)
     ]
-    level1 = [
-        along(PTS_DOWN, pts, p2.at[1], -2, even, even),
-        along(PTS_DOWN, pts, p2.at[1], -4, odd, odd),
-        along(PTS_UP2, pts, p2.at[0], 2, even, even),
-    ]
-    for copy in level1:
-        copy.start()
+    strip(1)
 
     for copy in c_t2:
         copy.wait_recv()
@@ -439,11 +434,14 @@
         copy.wait_recv()
     w1_own[...] = whole(w1_parts)
     c_w1 = send(W1, w1_own, w1_next, next1, out1, into1)
-    for k in range(strips):
-        strip_copy(1, k).wait_recv()
-    c_forward = send(FORWARD, p8.at[1], p8.at[2], at(32), meet_next, meet_last)
-    c_down1 = along(PTS_DOWN1, pts, p1, -1).start()
-    c_labels = along(LABELS, labels_in, labels_r, 1).start()
+    level1 = [
+        along(PTS_DOWN, pts, p2.at[1], -2, even, even),
+        along(PTS_DOWN, pts, p2.at[1], -4, odd, odd),
+        along(PTS_UP2, pts, p2.at[0], 2, even, even),
+    ]
+    for copy in level1:
+        copy.start()
+
 
     c_shift2.wait_recv()
     c_share_next = [
@@ -458,7 +456,15 @@
         for j in range(3)
     ]
 
+
+    for k in range(strips):
+        strip_copy(1, k).wait_recv()
+    c_forward = send(FORWARD, p8.at[1], p8.at[2], at(32), meet_next, meet_last)
+    c_down1 = along(PTS_DOWN1, pts, p1, -1).start()
+    c_labels = along(LABELS, labels_in, labels_r, 1).start()
     docs_copy(0).start()
+    docs_copy(1).start()
+    docs_copy(2).start()
 
     for copy in c_share2 + c_share_next:
         copy.wait_recv()
@@ -505,10 +511,6 @@
         ret2(2, 0, from_b - 32, meet_last, b_next),
         ret2(3, 1, from_a, meet_last, a_last),
     ]
-
-    @pl.loop(1, pieces)
-    def _(i):
-        docs_copy(i).start()
 
     c_down1.wait_recv()
     c_w0.wait_recv()

time: 102 us -> 89.1 us (0.87)
  the two profiles are of different devices: /device:TPU:25 before, /device:TPU:24 now
where the time goes in v5:
time: 89.1 us; the launch traced here: 87.8 us
  Pallas kernels  86.1 us (97%)
  local copies, waits for them, and re-layouts  1.77 us (2%)
    pallas_call x1, Pallas kernels, local(): pl.pallas_call(functools.partial(kernel, n), out_shape=jax.ShapeDtypeStru...  86.1 us

profile of v5, /device:TPU:24, one launch (start us, length us, event | category | flops | bytes accessed | tf_op | source)
XLA Modules:
  0.0 87.8 jit_solution(5116537153288701745)
XLA Ops:
  0.0 86.1 %shard_map.82 = f32[768,128]{1,0:T(8,128)} custom-call(bf16[768,1024]{1,0:T(8,128)(2,1)} %docs_hbm.1, bf16[768,128]{1,0:T(8,128)(2,1)} %labels_hbm.1, bf16[256,1024]{1,0:T(8,128)(2,1)} %skel_hbm.1, f32[2,4,256,256]{3,2,1,0:T(8,128)} %transfer_hbm.1, s32[1,2]{1,0:T(1,128)} %near_peer_hbm.1, s32[1,2]{1,0:T(1,128)} %near_live_hbm.1, s32[1,2,3]{2,1,0:T(2,128)} %bitcast.2, ...), custom_call_target="tpu_custom_call" | custom-call | tf_op jit(solution)/shard_map/pallas_call | solution.py:648
  86.1 1.8 %copy.10 = f32[768,128]{1,0:T(8,128)} copy(f32[768,128]{1,0:T(8,128)} %shard_map.82) | data formatting | bytes 786432

commit v6 on v5

--- a/solution.py
+++ b/solution.py
@@ -605,17 +605,15 @@
     down_low = (down - down_high.astype(f32)).astype(bf16)
     far = dot_nt(down_high, leaf[...]) + dot_nt(down_low, leaf[...])
 
+    near_t[...] += near_before * before_t[...] + (far_gain / rank) * far
+    width = labels_in.shape[1]
+
     @pl.loop(0, pieces)
     def _(i):
         rows = piece(i)
         near_copy(i).wait_recv()
-        near_t[:, rows] += (
-            near_before * before_t[:, rows] + near_after * near_recv[i].astype(f32)
-        )
-
-    total = near_t[...] + (far_gain / rank) * far
-    width = labels_in.shape[1]
-    out_ref[...] = (total[:width] / total[width : width + 1]).T
+        total = near_t[:, rows] + near_after * near_recv[i].astype(f32)
+        out_ref[rows, :] = (total[:width] / total[width : width + 1]).T
 
     for copies in (
         [c_down1, c_labels, c_w0, c_w1, c_shift2, c_ret0],

time: 89.1 us -> 89.2 us (level)
  no operation moved by 1% of the time
where the time goes in v6:
time: 89.2 us; the launch traced here: 87.9 us
  Pallas kernels  86.1 us (97%)
  local copies, waits for them, and re-layouts  1.77 us (2%)
    pallas_call x1, Pallas kernels, local(): pl.pallas_call(functools.partial(kernel, n), out_shape=jax.ShapeDtypeStru...  86.1 us

profile of v6, /device:TPU:24, one launch (start us, length us, event | category | flops | bytes accessed | tf_op | source)
XLA Modules:
  0.0 87.9 jit_solution(13911572311664087412)
XLA Ops:
  0.0 86.1 %shard_map.82 = f32[768,128]{1,0:T(8,128)} custom-call(bf16[768,1024]{1,0:T(8,128)(2,1)} %docs_hbm.1, bf16[768,128]{1,0:T(8,128)(2,1)} %labels_hbm.1, bf16[256,1024]{1,0:T(8,128)(2,1)} %skel_hbm.1, f32[2,4,256,256]{3,2,1,0:T(8,128)} %transfer_hbm.1, s32[1,2]{1,0:T(1,128)} %near_peer_hbm.1, s32[1,2]{1,0:T(1,128)} %near_live_hbm.1, s32[1,2,3]{2,1,0:T(2,128)} %bitcast.2, ...), custom_call_target="tpu_custom_call" | custom-call | tf_op jit(solution)/shard_map/pallas_call | solution.py:646
  86.2 1.8 %copy.10 = f32[768,128]{1,0:T(8,128)} copy(f32[768,128]{1,0:T(8,128)} %shard_map.82) | data formatting | bytes 786432
